TPU v7x, 128 devices: a whole 4x4x4 slice. The times are simulated.
128 devices in a mesh: dom: 32 (over z, y, core), head: 4 (over x).
Axes of the slice: x: 4, y: 4, z: 4, core: 2. Of those that a mesh axis runs over, the one named last changes fastest.
Arguments:
- features: bfloat16 [131072, 128], P('dom'), may hold values from -20 to 20
- qkv_weight: bfloat16 [128, 3, 128], P(None, None, 'head'), may hold values from -0.5 to 0.5
- out_weight: bfloat16 [128, 128], replicated, may hold values from -0.5 to 0.5
- ffn_in: bfloat16 [128, 256], P(None, 'head'), may hold values from -0.5 to 0.5
- ffn_out: bfloat16 [256, 128], P('head'), may hold values from -0.375 to 0.375
- norm_gains: float32 [2, 128], replicated, may hold values from 0.25 to 1.75
- virtual_table: bfloat16 [8, 128], replicated, may hold values from -6 to 6
- block_mask: int32 [131072, 128], P('dom'), may hold values 0 or 1
- halo_send: int32 [32, 2, 2048], P('dom'), may hold values from 0 to 4095
- halo_links: int32 [131072, 4], P('dom'), may hold values from 0 to 4095
- expander_perm: int32 [3, 32, 4096], P(None, 'dom'), may hold values from 0 to 4095, each once within a row
- virtual_ids: int32 [131072], P('dom'), may hold values from 0 to 7
Outputs:
- layer_out: bfloat16 [131072, 128], P(('dom', 'head'))
All inputs are finite; a program needn't handle non-finite values. No bound on the sum of `block_mask` on one device may be relied on, other than what follows from the above.
Results may differ from a plain program's by a relative error of at most 0.015.
Values may be sent and summed in bfloat16 or wider, within the bound.
A program may use at most 64 MiB of HBM per device.

v0:
```python
import jax
import jax.numpy as jnp
from jax import lax
from jax.sharding import PartitionSpec as P

HEAD_DIM = 16
BLOCK = 128


def passed_along(array, axis, by):
    count = lax.axis_size(axis)
    return lax.ppermute(array, axis, [(i, (i + by) % count) for i in range(count)])


def from_partner(block, axis, stride):
    count = lax.axis_size(axis)
    route = []
    for low in range(count):
        high = low | 1 << stride
        if high != low and high < count:
            route += [(low, high), (high, low)]
    return lax.ppermute(block, axis, route)


def layer_norm(values_in, gain):
    center = jnp.mean(values_in, axis=-1, keepdims=True)
    shifted = values_in - center
    second = jnp.mean(shifted * shifted, axis=-1, keepdims=True)
    return shifted * lax.rsqrt(second + 1e-05) * gain


def pick_rows(indices, table):
    return jnp.take(table, indices, axis=0)


def attend(queries, key_rows, value_rows, allowed, group_keys, group_values):
    node_count, local_width = queries.shape
    head_count = local_width // HEAD_DIM
    block_count = node_count // BLOCK
    scale = HEAD_DIM ** (-0.5)
    q_blocks = queries.reshape(block_count, BLOCK, head_count, HEAD_DIM)
    k_blocks = key_rows.reshape(block_count, BLOCK, head_count, HEAD_DIM)
    v_blocks = value_rows.reshape(block_count, BLOCK, head_count, HEAD_DIM)
    near_scores = (
        jnp.einsum("bihd,bjhd->bihj", q_blocks, k_blocks, preferred_element_type=jnp.float32)
        * scale
    )
    near_scores = jnp.where(
        allowed[:, None, :], near_scores.reshape(node_count, head_count, BLOCK), -1e30
    )
    q_nodes = queries.reshape(node_count, head_count, HEAD_DIM)
    group_scores = []
    for group in group_keys:
        count = group.shape[1]
        keys_here = group.reshape(node_count, count, head_count, HEAD_DIM)
        group_scores.append(
            jnp.einsum("nhd,nehd->nhe", q_nodes, keys_here, preferred_element_type=jnp.float32)
            * scale
        )
    row_max = jnp.max(near_scores, axis=-1, keepdims=True)
    for scored in group_scores:
        row_max = jnp.maximum(row_max, jnp.max(scored, axis=-1, keepdims=True))
    near_exp = jnp.exp(near_scores - row_max)
    group_exp = [jnp.exp(scored - row_max) for scored in group_scores]
    row_total = jnp.sum(near_exp, axis=-1, keepdims=True)
    for expd in group_exp:
        row_total = row_total + jnp.sum(expd, axis=-1, keepdims=True)
    near_weights = (
        (near_exp / row_total).astype(jnp.bfloat16).reshape(block_count, BLOCK, head_count, BLOCK)
    )
    combined = jnp.einsum(
        "bihj,bjhd->bihd", near_weights, v_blocks, preferred_element_type=jnp.float32
    )
    combined = combined.reshape(node_count, head_count, HEAD_DIM)
    for expd, group in zip(group_exp, group_values):
        count = group.shape[1]
        weights = (expd / row_total).astype(jnp.bfloat16)
        values_here = group.reshape(node_count, count, head_count, HEAD_DIM)
        combined = combined + jnp.einsum(
            "nhe,nehd->nhd", weights, values_here, preferred_element_type=jnp.float32
        )
    return combined.reshape(node_count, local_width).astype(jnp.bfloat16)


def per_device(
    features,
    qkv_weight,
    out_weight,
    ffn_in,
    ffn_out,
    norm_gains,
    virtual_table,
    block_mask,
    halo_send,
    halo_links,
    expander_perm,
    virtual_ids,
):
    node_count, model_width = features.shape
    local_width = qkv_weight.shape[2]
    projected = jnp.dot(
        features,
        qkv_weight.reshape(model_width, 3 * local_width),
        preferred_element_type=jnp.float32,
    ).astype(jnp.bfloat16)
    queries = projected[:, :local_width]
    key_value = projected[:, local_width:]
    virtual_kv = jnp.dot(
        virtual_table,
        qkv_weight[:, 1:].reshape(model_width, 2 * local_width),
        preferred_element_type=jnp.float32,
    ).astype(jnp.bfloat16)
    from_below = passed_along(pick_rows(halo_send[0, 1], key_value), "dom", 1)
    from_above = passed_along(pick_rows(halo_send[0, 0], key_value), "dom", -1)
    halo_rows = jnp.concatenate([from_below, from_above], axis=0)
    link_count = halo_links.shape[1]
    linked = pick_rows(halo_links.reshape(node_count * link_count), halo_rows).reshape(
        node_count, link_count, 2 * local_width
    )
    levels = lax.axis_size("dom").bit_length() - 1
    partner_list = []
    for matching in range(3):
        partner_rows = from_partner(key_value, "dom", matching * (levels - 1) // 2)
        partner_list.append(pick_rows(expander_perm[matching, 0], partner_rows))
    paired = jnp.stack(partner_list, axis=1)
    hub_rows = pick_rows(virtual_ids, virtual_kv)[:, None, :]
    position = jnp.arange(node_count, dtype=jnp.int32) % BLOCK
    allowed = (block_mask > 0) | (position[:, None] == jnp.arange(BLOCK, dtype=jnp.int32)[None, :])
    group_keys = [linked[..., :local_width], paired[..., :local_width], hub_rows[..., :local_width]]
    group_values = [
        linked[..., local_width:],
        paired[..., local_width:],
        hub_rows[..., local_width:],
    ]
    attended = attend(
        queries,
        key_value[:, :local_width],
        key_value[:, local_width:],
        allowed,
        group_keys,
        group_values,
    )
    head_index = lax.axis_index("head")
    quarter = node_count // lax.axis_size("head")
    mixed_out = jnp.dot(
        lax.all_gather(attended, "head", axis=1, tiled=True),
        out_weight,
        preferred_element_type=jnp.float32,
    )
    hidden_in = layer_norm(features.astype(jnp.float32) + mixed_out, norm_gains[0]).astype(
        jnp.bfloat16
    )
    inner = jax.nn.gelu(
        jnp.dot(hidden_in, ffn_in, preferred_element_type=jnp.float32), approximate=True
    ).astype(jnp.bfloat16)
    partial_out = jnp.dot(inner, ffn_out, preferred_element_type=jnp.float32)
    summed = lax.psum_scatter(
        partial_out.astype(jnp.bfloat16), "head", scatter_dimension=0, tiled=True
    ).astype(jnp.float32)
    residual = lax.dynamic_slice_in_dim(hidden_in, head_index * quarter, quarter, 0)
    return layer_norm(residual.astype(jnp.float32) + summed, norm_gains[1]).astype(jnp.bfloat16)


def solution(mesh):
    return jax.shard_map(
        per_device,
        mesh=mesh,
        in_specs=(
            P("dom", None),
            P(None, None, "head"),
            P(),
            P(None, "head"),
            P("head", None),
            P(),
            P(),
            P("dom", None),
            P("dom", None, None),
            P("dom", None),
            P(None, "dom", None),
            P("dom"),
        ),
        out_specs=P(("dom", "head"), None),
        check_vma=False,
    )
```

profile of v0, /device:TPU:0, one launch (start us, length us, event | category | flops | bytes accessed | tf_op | source)
XLA Modules:
  0.0 270.5 jit_solution(4711288207603556996)
XLA Ops:
  6.5 1.7 convolution_convert_fusion.1
  8.3 0.9 slice.91
  9.1 4.0 %collective-permute-start.4 = (bf16[4096,64]{0,1:T(8,128)(2,1)}, bf16[4096,64]{0,1:T(8,128)(2,1)}, u32[]{:S(2)}, u32[]{:S(2)}) collective-permute-start(bf16[4096,64]{0,1:T(8,128)(2,1)} %slice.91), channel_id=1, source_target_pairs={{0,64},{64,0},{4,68},{68,4},{8,72},{72,8},{12,76},{76,12},{16,80},... | collective-permute-start | bytes 1572872 | tf_op jit(solution)/shard_map/ppermute | solution.py:22
  13.1 3.2 %collective-permute-start.3 = (bf16[4096,64]{0,1:T(8,128)(2,1)}, bf16[4096,64]{0,1:T(8,128)(2,1)}, u32[]{:S(2)}, u32[]{:S(2)}) collective-permute-start(bf16[4096,64]{0,1:T(8,128)(2,1)} %slice.91), channel_id=1, source_target_pairs={{0,16},{16,0},{4,20},{20,4},{8,24},{24,8},{12,28},{28,12},{32,48},... | collective-permute-start | bytes 1572872 | tf_op jit(solution)/shard_map/ppermute | solution.py:22
  16.3 1.5 copy.105
  17.9 6.2 %gather_fusion.3 = bf16[2048,64]{1,0:T(8,128)(2,1)S(1)} fusion(bf16[4096,64]{1,0:T(8,128)(2,1)S(1)} %copy.105, s32[2048]{0:T(1024)S(1)} %fusion.45), kind=kCustom, calls=%fused_computation.2.clone | custom fusion | bytes 532480 | tf_op jit(solution)/shard_map/jit(_take)/gather | solution.py:33
  24.1 1.1 broadcast_select_fusion.1
  25.2 1.3 collective-permute-start.1
  26.6 6.2 %gather_fusion.2 = bf16[2048,64]{1,0:T(8,128)(2,1)S(1)} fusion(bf16[4096,64]{1,0:T(8,128)(2,1)S(1)} %copy.105, s32[2048]{0:T(1024)S(1)} %fusion.44), kind=kCustom, calls=%fused_computation.clone | custom fusion | bytes 532480 | tf_op jit(solution)/shard_map/jit(_take)/gather | solution.py:33
  32.8 1.1 broadcast_select_fusion.2
  33.9 0.6 fusion.42
  34.5 0.6 compare_and_fusion.1
  35.1 0.6 fusion.41
  35.7 0.6 compare_and_fusion.2
  36.3 0.9 slice_bitcast_fusion.1
  37.2 0.6 copy.107
  37.9 0.6 compare_and_fusion
  38.5 0.6 add_select_fusion
  39.1 0.6 slice.67
  39.7 1.3 fusion.39
  41.1 1.3 compare_and_fusion.4
  42.4 0.6 compare_and_fusion.3
  43.0 1.7 reshape.222
  44.9 3.5 %fusion.2 = pred[4096,128]{1,0:T(8,128)(4,1)S(1)} fusion(s32[4096,128]{1,0:T(8,128)} %param.23, s32[4096]{0:T(1024)} %add_select_fusion), kind=kLoop, calls=%fused_computation.21 | loop fusion | flops 1572864 | bytes 2637824 | tf_op jit(solution)/shard_map/or | solution.py:128
  48.4 1.0 copy.102
  49.4 0.8 copy.164
  50.2 0.7 copy.163
  51.0 12.1 %gather_fusion.1 = bf16[4096,64]{1,0:T(8,128)(2,1)S(1)} fusion(bf16[8,64]{1,0:T(8,128)(2,1)S(1)} %convolution_convert_fusion.2, s32[4096]{0:T(1024)S(1)} %copy-done.22), kind=kCustom, calls=%fused_computation.6 | custom fusion | bytes 1064960 | tf_op jit(solution)/shard_map/jit(_take)/gather | solution.py:33
  63.6 0.7 fusion.55
  64.6 3.6 %fusion.1 = (f32[32,128,2]{1,2,0:T(2,128)}, f32[32,2,128,128]{3,2,1,0:T(8,128)}) fusion(pred[32,128,128]{1,2,0:T(8,128)(4,1)S(1)} %copy.102, bf16[32,128,2,16]{1,0,3,2:T(8,128)(2,1)S(1)} %bitcast.120, bf16[32,128,2,16]{1,0,3,2:T(8,128)(2,1)S(1)} %bitcast.121), kind=kOutput, calls=%fused_computation.14 | convolution fusion | flops 36691968 | bytes 5275648 | tf_op jit(solution)/shard_map/bihd,bjhd->bihj/dot_general | solution.py:45
  68.4 0.7 copy.162
  69.1 0.6 fusion.40
  69.7 1.4 pad_maximum_fusion.1
  71.1 57.4 %gather_fusion = bf16[16384,64]{1,0:T(8,128)(2,1)} fusion(bf16[4096,64]{1,0:T(8,128)(2,1)S(1)} %pad_maximum_fusion.1, s32[16384]{0:T(1024)S(1)} %broadcast_clamp_fusion), kind=kCustom, calls=%fused_computation.5 | custom fusion | bytes 4259840 | tf_op jit(solution)/shard_map/jit(_take)/gather | solution.py:33
  128.5 5.6 %copy.108 = bf16[4096,4,64]{0,2,1:T(8,128)(2,1)S(1)} copy(bf16[4096,4,64]{2,1,0:T(4,128)(2,1)} %bitcast.109) | data formatting | bytes 4194304 | tf_op jit(solution)/shard_map/jit(_take)/gather | solution.py:33
  134.4 1.2 fusion.54
  135.6 0.5 multiply_reduce_fusion.1
  136.2 1.5 copy.111
  137.8 12.1 %gather_fusion.6 = bf16[4096,64]{1,0:T(8,128)(2,1)S(1)} fusion(bf16[4096,64]{1,0:T(8,128)(2,1)S(1)} %copy.111, s32[4096]{0:T(1024)S(1)} %copy-done.20), kind=kCustom, calls=%fused_computation.4.clone | custom fusion | bytes 1064960 | tf_op jit(solution)/shard_map/jit(_take)/gather | solution.py:33
  149.9 1.5 copy.110
  151.5 14.9 %gather_fusion.5 = bf16[4096,64]{1,0:T(8,128)(2,1)} fusion(bf16[4096,64]{1,0:T(8,128)(2,1)S(1)} %copy.110, s32[4096]{0:T(1024)S(1)} %copy-done.19), kind=kCustom, calls=%fused_computation.3.clone | custom fusion | bytes 1064960 | tf_op jit(solution)/shard_map/jit(_take)/gather | solution.py:33
  166.4 1.5 copy.109
  167.9 12.1 %gather_fusion.4 = bf16[4096,64]{1,0:T(8,128)(2,1)S(1)} fusion(bf16[4096,64]{1,0:T(8,128)(2,1)S(1)} %copy.109, s32[4096]{0:T(1024)S(1)} %copy-done.21), kind=kCustom, calls=%fused_computation.1.clone | custom fusion | bytes 1064960 | tf_op jit(solution)/shard_map/jit(_take)/gather | solution.py:33
  180.1 2.1 select_bitcast_fusion.2
  182.3 1.4 select_bitcast_fusion
  183.7 0.8 pad_maximum_fusion
  184.4 2.7 %fusion.53 = (bf16[4096,3,32]{2,0,1:T(8,128)(2,1)}, bf16[4096,3,32]{2,0,1:T(8,128)(2,1)S(1)}) fusion(bf16[4096,3,64]{2,0,1:T(8,128)(2,1)S(1)} %pad_maximum_fusion), kind=kLoop, calls=%fused_computation.126 | loop fusion | bytes 3145728 | tf_op jit(solution)/shard_map/slice | solution.py:129
  187.2 4.0 %copy.152 = bf16[4096,3,32]{0,2,1:T(8,128)(2,1)} copy(bf16[4096,3,32]{2,0,1:T(8,128)(2,1)} %get-tuple-element.9) | data formatting | bytes 1572864
  191.2 1.7 multiply_reduce_fusion.4
  193.3 3.4 %fusion = f32[32,128,2]{1,2,0:T(2,128)S(1)} fusion(f32[32,2,128,128]{3,2,1,0:T(8,128)} %get-tuple-element.27, f32[32,128,2]{1,2,0:T(2,128)S(1)} %bitcast.113, pred[32,128,128]{1,2,0:T(8,128)(4,1)S(1)} %copy-done.6), kind=kLoop, calls=%fused_computation.13 | loop fusion | flops 4186112 | bytes 4784128 | tf_op jit(solution)/shard_map/reduce_sum | solution.py:65
  196.8 0.7 fusion.30
  197.6 2.4 copy.154
  200.2 1.5 multiply_reduce_fusion.3
  201.9 3.4 %fusion.4 = f32[32,2,2,8,128]{4,3,2,1,0:T(8,128)S(1)} fusion(f32[32,2,128,128]{3,2,1,0:T(8,128)} %get-tuple-element.27, f32[32,128,2]{1,2,0:T(2,128)S(1)} %bitcast.118, f32[32,128,2]{1,2,0:T(2,128)S(1)} %bitcast.114, pred[32,128,128]{1,2,0:T(8,128)(4,1)S(1)} %copy-done.7, bf16[32,128,2,16]{1,0,3,2:T(8,128)(2,1)S(1)} %bitcast.119), kind=kOutput, calls=%fused_computation.27 | convolution fusion | flops 38797312 | bytes 5570560 | tf_op jit(solution)/shard_map/bihj,bjhd->bihd/dot_general | solution.py:71
  205.4 0.9 fusion.16
  206.7 0.5 copy.101
  207.2 23.9 %all-gather.2.cloned.1.call-done = bf16[4096,128]{0,1:T(8,128)(2,1)} async-done(((bf16[4096,32]{0,1:T(8,128)(2,1)}), bf16[4096,128]{0,1:T(8,128)(2,1)}) %all-gather.2.cloned.1.call-update) | async-done | bytes 1048592 | tf_op jit(solution)/shard_map/all_gather | solution.py:146
  231.2 1.7 fusion.58
  233.9 1.7 convolution_convert_fusion
  235.7 24.0 %reduce-scatter.2.cloned.1.call-done = bf16[1024,128]{0,1:T(8,128)(2,1)} async-done(((bf16[4096,128]{0,1:T(8,128)(2,1)}), bf16[1024,128]{0,1:T(8,128)(2,1)}) %reduce-scatter.2.cloned.1.call-update) | async-done | bytes 262160 | tf_op jit(solution)/shard_map/reduce_scatter | solution.py:157
  259.6 1.0 fusion.22
  260.7 1.1 multiply_reduce_fusion.6
  261.8 1.1 multiply_convert_fusion.1
  262.9 0.8 copy.121
  (110 shorter events, 3.9 us)
Async XLA Ops:
  6.5 224.6 %copy-start = (bf16[128,128]{1,0:T(8,128)(2,1)S(1)}, bf16[128,128]{1,0:T(8,128)(2,1)}, u32[]{:S(2)}) copy-start(bf16[128,128]{1,0:T(8,128)(2,1)} %param.18) | copy-start | bytes 98308
  6.5 224.6 %all-gather.2.cloned.1.call-start = ((), (), s32[]{:S(2)}) async-start(), calls=%async_computation.1 | async-start | bytes 1310720 | tf_op jit(solution)/shard_map/all_gather | solution.py:146
  6.5 11.3 %copy-start.28 = (s32[1,2,2048]{2,1,0:T(2,128)S(1)}, s32[1,2,2048]{2,1,0:T(2,128)}, u32[]{:S(2)}) copy-start(s32[1,2,2048]{2,1,0:T(2,128)} %param.24) | copy-start | bytes 49156
  9.1 127.1 %collective-permute-start.4 = (bf16[4096,64]{0,1:T(8,128)(2,1)}, bf16[4096,64]{0,1:T(8,128)(2,1)}, u32[]{:S(2)}, u32[]{:S(2)}) collective-permute-start(bf16[4096,64]{0,1:T(8,128)(2,1)} %slice.91), channel_id=1, source_target_pairs={{0,64},{64,0},{4,68},{68,4},{8,72},{72,8},{12,76},{76,12},{16,80},... | collective-permute-start | bytes 1572872 | tf_op jit(solution)/shard_map/ppermute | solution.py:22
  13.1 136.8 %collective-permute-start.3 = (bf16[4096,64]{0,1:T(8,128)(2,1)}, bf16[4096,64]{0,1:T(8,128)(2,1)}, u32[]{:S(2)}, u32[]{:S(2)}) collective-permute-start(bf16[4096,64]{0,1:T(8,128)(2,1)} %slice.91), channel_id=1, source_target_pairs={{0,16},{16,0},{4,20},{20,4},{8,24},{24,8},{12,28},{28,12},{32,48},... | collective-permute-start | bytes 1572872 | tf_op jit(solution)/shard_map/ppermute | solution.py:22
  16.3 150.1 %collective-permute-start.2 = (bf16[4096,64]{0,1:T(8,128)(2,1)}, bf16[4096,64]{0,1:T(8,128)(2,1)}, u32[]{:S(2)}, u32[]{:S(2)}) collective-permute-start(bf16[4096,64]{0,1:T(8,128)(2,1)} %slice.91), channel_id=1, source_target_pairs={{0,4},{4,0},{8,12},{12,8},{16,20},{20,16},{24,28},{28,24},{32,36},... | collective-permute-start | bytes 1572872 | tf_op jit(solution)/shard_map/ppermute | solution.py:22
  25.2 44.5 %collective-permute-start.1 = (bf16[2048,64]{1,0:T(8,128)(2,1)}, bf16[2048,64]{1,0:T(8,128)(2,1)}, u32[]{:S(2)}, u32[]{:S(2)}) collective-permute-start(bf16[2048,64]{1,0:T(8,128)(2,1)} %broadcast_select_fusion.1), channel_id=1, source_target_pairs={{0,124},{4,0},{8,4},{12,8},{16,12},{20,16},{24,20},{28,24},{32,28}... | collective-permute-start | bytes 786440 | tf_op jit(solution)/shard_map/ppermute | solution.py:12
  26.5 7.3 %copy-start.24 = (s32[3,1,4096]{2,1,0:T(1,128)S(1)}, s32[3,1,4096]{2,1,0:T(1,128)}, u32[]{:S(2)}) copy-start(s32[3,1,4096]{2,1,0:T(1,128)} %param.26) | copy-start | bytes 147460
  32.7 4.5 %copy-start.13 = (s32[4096,4]{0,1:T(4,128)S(1)}, s32[4096,4]{0,1:T(4,128)}, u32[]{:S(2)}) copy-start(s32[4096,4]{0,1:T(4,128)} %param.25) | copy-start | bytes 196612
  33.9 35.8 %collective-permute-start = (bf16[2048,64]{1,0:T(8,128)(2,1)}, bf16[2048,64]{1,0:T(8,128)(2,1)}, u32[]{:S(2)}, u32[]{:S(2)}) collective-permute-start(bf16[2048,64]{1,0:T(8,128)(2,1)} %broadcast_select_fusion.2), channel_id=1, source_target_pairs={{0,4},{4,8},{8,12},{12,16},{16,20},{20,24},{24,28},{28,32},{32,36}... | collective-permute-start | bytes 786440 | tf_op jit(solution)/shard_map/ppermute | solution.py:12
  36.3 2.8 %copy-start.17 = (bf16[128,3,32]{0,2,1:T(8,128)(2,1)S(1)}, bf16[128,3,32]{0,2,1:T(8,128)(2,1)}, u32[]{:S(2)}) copy-start(bf16[128,3,32]{0,2,1:T(8,128)(2,1)} %param.17) | copy-start | bytes 73732
  37.2 98.3 %copy-start.1 = (f32[4096,2,16]{0,2,1:T(8,128)}, f32[4096,2,16]{0,2,1:T(8,128)S(1)}, u32[]{:S(2)}) copy-start(f32[4096,2,16]{0,2,1:T(8,128)S(1)} %get-tuple-element.14) | copy-start | bytes 1572868
  44.7 4.6 %copy-start.10 = (bf16[4,8,32,128]{3,1,2,0:T(8,128)(2,1)S(1)}, bf16[4,8,32,128]{3,1,2,0:T(8,128)(2,1)}, u32[]{:S(2)}) copy-start(bf16[4,8,32,128]{3,1,2,0:T(8,128)(2,1)} %get-tuple-element.15) | copy-start | bytes 786436
  44.8 5.3 %copy-start.9 = (bf16[4,8,32,128]{3,1,2,0:T(8,128)(2,1)S(1)}, bf16[4,8,32,128]{3,1,2,0:T(8,128)(2,1)}, u32[]{:S(2)}) copy-start(bf16[4,8,32,128]{3,1,2,0:T(8,128)(2,1)} %get-tuple-element.16) | copy-start | bytes 786436
  44.8 6.1 %copy-start.23 = (bf16[128,2,32]{0,2,1:T(8,128)(2,1)S(1)}, bf16[128,2,32]{0,2,1:T(8,128)(2,1)}, u32[]{:S(2)}) copy-start(bf16[128,2,32]{0,2,1:T(8,128)(2,1)} %slice.67) | copy-start | bytes 49156
  44.8 6.1 %copy-start.31 = (bf16[8,128]{1,0:T(8,128)(2,1)S(1)}, bf16[8,128]{1,0:T(8,128)(2,1)}, u32[]{:S(2)}) copy-start(bf16[8,128]{1,0:T(8,128)(2,1)} %param.22) | copy-start | bytes 6148
  44.9 6.2 %copy-start.22 = (s32[4096]{0:T(1024)S(1)}, s32[4096]{0:T(1024)}, u32[]{:S(2)}) copy-start(s32[4096]{0:T(1024)} %fusion.39) | copy-start | bytes 49156
  49.3 15.0 %copy-start.5 = (pred[32,128,128]{1,2,0:T(8,128)(4,1)}, pred[32,128,128]{1,2,0:T(8,128)(4,1)S(1)}, u32[]{:S(2)}) copy-start(pred[32,128,128]{1,2,0:T(8,128)(4,1)S(1)} %copy.102) | copy-start | bytes 1572868
  51.0 12.5 %copy-start.27 = (pred[4096]{0:T(1024)(128)(4,1)S(1)}, pred[4096]{0:T(1024)(128)(4,1)}, u32[]{:S(2)}) copy-start(pred[4096]{0:T(1024)(128)(4,1)} %compare_and_fusion.4) | copy-start | bytes 12292
  63.5 1.0 copy-start.15
  63.5 1.1 copy-start.16
  64.6 3.7 %copy-start.8 = (bf16[4,8,32,128]{3,1,2,0:T(8,128)(2,1)S(1)}, bf16[4,8,32,128]{3,1,2,0:T(8,128)(2,1)}, u32[]{:S(2)}) copy-start(bf16[4,8,32,128]{3,1,2,0:T(8,128)(2,1)} %get-tuple-element.13) | copy-start | bytes 786436
  128.5 5.6 %copy-start.18 = (pred[4096,4]{0,1:T(4,128)(4,1)S(1)}, pred[4096,4]{0,1:T(4,128)(4,1)}, u32[]{:S(2)}) copy-start(pred[4096,4]{0,1:T(4,128)(4,1)} %compare_and_fusion) | copy-start | bytes 49156
  135.6 2.2 copy-start.20
  137.8 13.7 %copy-start.19 = (s32[4096]{0:T(1024)S(1)}, s32[4096]{0:T(1024)}, u32[]{:S(2)}) copy-start(s32[4096]{0:T(1024)} %fusion.41) | copy-start | bytes 49156
  151.5 16.4 %copy-start.21 = (s32[4096]{0:T(1024)S(1)}, s32[4096]{0:T(1024)}, u32[]{:S(2)}) copy-start(s32[4096]{0:T(1024)} %fusion.40) | copy-start | bytes 49156
  167.9 12.2 %copy-start.26 = (pred[4096]{0:T(1024)(128)(4,1)S(1)}, pred[4096]{0:T(1024)(128)(4,1)}, u32[]{:S(2)}) copy-start(pred[4096]{0:T(1024)(128)(4,1)} %compare_and_fusion.3) | copy-start | bytes 12292
  180.0 2.2 copy-start.3
  180.1 2.2 copy-start.29
  180.1 2.2 copy-start.30
  187.2 5.8 %copy-start.25 = (f32[32,128,2]{1,2,0:T(2,128)S(1)}, f32[32,128,2]{1,2,0:T(2,128)}, u32[]{:S(2)}) copy-start(f32[32,128,2]{1,2,0:T(2,128)} %get-tuple-element.26) | copy-start | bytes 98308
  191.2 2.1 copy-start.6
  197.6 2.5 copy-start.12
  200.1 1.6 copy-start.4
  200.1 1.9 copy-start.7
  200.1 1.9 copy-start.14
  201.9 3.4 %copy-start.11 = (bf16[4096,1,32]{0,2,1:T(8,128)(2,1)S(1)}, bf16[4096,1,32]{0,2,1:T(8,128)(2,1)}, u32[]{:S(2)}) copy-start(bf16[4096,1,32]{0,2,1:T(8,128)(2,1)} %get-tuple-element.17) | copy-start | bytes 786436
  205.4 1.3 copy-start.2
  205.4 1.9 copy-start.32
  206.3 53.4 %reduce-scatter.2.cloned.1.call-start = ((), (), s32[]{:S(2)}) async-start(), calls=%async_computation.2 | async-start | bytes 1310720 | tf_op jit(solution)/shard_map/reduce_scatter | solution.py:157
  233.2 0.7 copy-start.33
  233.2 0.7 copy-start.34
Sparse Core Ops, SparseCore 0:
  206.4 24.7 all-gather.1
  235.8 23.7 reduce-scatter.1
where the time goes:
time: 271 us
  local copies, waits for them, and re-layouts  154 us (57%)
  waiting for transfers between devices  47.9 us (18%)
  other arithmetic  33.8 us (12%)
  between operations  14.1 us (5%)
  matrix products  12.3 us (5%)
  starting transfers between devices  8.49 us (3%)
    gather x9, local copies, waits for them, and re-layouts, pick_rows(): return jnp.take(table, indices, axis=0)  127 us
    reduce_scatter x1, waiting for transfers between devices, per_device(): lax.psum_scatter(partial_out.astype(jnp.bfloat16), 'head', scatter_dimens...  24 us
    all_gather x1, waiting for transfers between devices, per_device(): lax.all_gather(attended, 'head', axis=1, tiled=True)  23.9 us
    unnamed x78, local copies, waits for them, and re-layouts  11.1 us
    ppermute x3, starting transfers between devices, from_partner(): return lax.ppermute(block, axis, route)  7.16 us
  transfers between devices with their start and end apart: 7, of which 2 were waited for; matrix products, arithmetic and copies ran while one was open for 55% of the time, Pallas kernels for 0%

commit v1 on v0

v1 whole, which is shorter than its diff:
```python
import functools

import jax
import jax.numpy as jnp
from jax import lax
from jax.experimental import pallas as pl
from jax.experimental.pallas import tpu as pltpu
from jax.sharding import PartitionSpec as P

HEAD_DIM = 16
BLOCK = 128
ROWS = 64
MESH = pl.DeviceIdType.MESH
F32 = jnp.float32
BF16 = jnp.bfloat16


def dot_nt(a, b):
    return lax.dot_general(a, b, (((1,), (1,)), ((), ())), preferred_element_type=F32)


def dot_nn(a, b):
    return jnp.dot(a, b, preferred_element_type=F32)


def gather_rows(count, index_of, table, out, out_base):
    def step(i, carry):
        base = pl.multiple_of(i * ROWS, ROWS)
        for u in range(ROWS):
            out[pl.ds(out_base + base + u, 1), :] = table[pl.ds(index_of(base + u), 1), :]
        return carry

    lax.fori_loop(0, count // ROWS, step, 0)


def widen(source, out, out_base, rows):
    def step(i, carry):
        at = pl.multiple_of(i * 256, 256)
        out[pl.ds(pl.multiple_of(out_base + at, 256), 256), :] = source[pl.ds(at, 256), :].astype(F32)
        return carry

    lax.fori_loop(0, rows // 256, step, 0)


def exchange_kernel(
    n_dom,
    n_head,
    feats,
    send_smem,
    send_vmem,
    perm,
    wqkv,
    w1,
    w2,
    peer_feats,
    near_list,
    rows_a,
    rows_b,
    lookup,
    weights,
    table,
    staged,
    packed,
    wpack,
    peer_send,
    request,
    request_smem,
    feats_sems,
    send_sems,
    req_send,
    req_recv,
    list_send,
    list_recv,
    rows_send,
    rows_recv,
    w_send,
    w_recv,
    local_sem,
):
    nodes = feats.shape[0]
    halo = near_list.shape[0]
    part = rows_a.shape[0]
    dom = lax.axis_index("dom")
    head = lax.axis_index("head")
    core = lax.rem(dom, 2)
    peer = dom + 1 - 2 * core
    side = lax.rem(dom + 2 * core - 1 + n_dom, n_dom)
    levels = n_dom.bit_length() - 1

    def flipped(stride):
        bit = lax.rem(dom // (1 << stride), 2)
        return dom + (1 - 2 * bit) * (1 << stride)

    partners = [flipped(m * (levels - 1) // 2) for m in (1, 2)]
    others = [lax.rem(head + k, n_head) for k in range(1, n_head)]

    barrier = pltpu.get_barrier_semaphore()
    for dev in [peer, side] + partners:
        pl.semaphore_signal(barrier, inc=1, device_id={"dom": dev}, device_id_type=MESH)
    for dev in others:
        pl.semaphore_signal(barrier, inc=1, device_id={"head": dev}, device_id_type=MESH)
    pl.semaphore_wait(barrier, 4 + len(others))

    def remote(src, dst, send, recv, device):
        return pltpu.make_async_remote_copy(
            src_ref=src, dst_ref=dst, send_sem=send, recv_sem=recv, device_id=device, device_id_type=MESH
        )

    started = []
    for m in (0, 1):
        copy = remote(
            perm.at[m + 1, 0, pl.ds(pl.multiple_of(head * part, 128), part)],
            request.at[m],
            req_send.at[m],
            req_recv.at[m],
            {"dom": partners[m]},
        )
        copy.start()
        started.append(copy)
    requests = list(started)
    send_copy = remote(send_vmem, peer_send, send_sems.at[0], send_sems.at[1], {"dom": peer})
    send_copy.start()
    feats_copy = remote(feats, peer_feats, feats_sems.at[0], feats_sems.at[1], {"dom": peer})
    feats_copy.start()

    q_rows, f_rows = wqkv.shape[0], w1.shape[0]
    wpack[0:q_rows, :] = wqkv[...]
    wpack[q_rows : q_rows + f_rows, :] = w1[...]
    wpack[q_rows + f_rows : q_rows + 2 * f_rows, :] = w2[...]
    w_copies = []
    for k, dev in enumerate(others):
        copy = remote(wpack, weights.at[head], w_send.at[k], w_recv.at[head], {"head": dev})
        copy.start()
        w_copies.append(copy)
    own = pltpu.make_async_copy(wpack, weights.at[head], local_sem.at[0])
    own.start()

    widen(feats, table, 0, nodes)

    chunk = staged.shape[0]

    def send_chunk(index_of, at, slot, dst, send, recv, device):
        gather_rows(chunk, index_of, table, staged, 0)
        packed[slot] = staged[...].astype(BF16)
        copy = remote(packed.at[slot], dst.at[pl.ds(at, chunk), :], send, recv, device)
        copy.start()
        return copy

    chunks = []
    slot = 0
    for i in range(halo // chunk):
        chunks.append(
            send_chunk(
                lambda r, i=i: send_smem[core, i * chunk + r],
                i * chunk,
                slot,
                near_list,
                list_send.at[i],
                list_recv.at[i],
                {"dom": side},
            )
        )
        slot += 1
    for m, dst in ((0, rows_a), (1, rows_b)):
        requests[m].wait_recv()
        moved = pltpu.make_async_copy(request.at[m], request_smem.at[m], local_sem.at[1 + m])
        moved.start()
        moved.wait()
        for i in range(part // chunk):
            k = m * (part // chunk) + i
            chunks.append(
                send_chunk(
                    lambda r, i=i, m=m: request_smem[m, i * chunk + r],
                    i * chunk,
                    slot,
                    dst,
                    rows_send.at[k],
                    rows_recv.at[k],
                    {"dom": partners[m]},
                )
            )
            slot += 1

    send_copy.wait()
    ramp = nodes + lax.broadcasted_iota(jnp.int32, (1, halo), 1)
    even = core == 0
    lookup[0:1, :] = jnp.where(even, ramp, peer_send[1:2, :])
    lookup[1:2, :] = jnp.where(even, peer_send[0:1, :], ramp)

    for copy in requests:
        copy.wait_send()
    feats_copy.wait()
    own.wait()
    for k, copy in enumerate(w_copies):
        copy.wait_send()
    for dev in others:
        remote(wpack, weights.at[dev], w_send.at[0], w_recv.at[dev], {"head": dev}).wait_recv()
    for copy in chunks:
        copy.wait()


def layer_norm_cols(values, gain):
    count = values.shape[0]
    center = jnp.sum(values, axis=0, keepdims=True) * (1.0 / count)
    shifted = values - center
    second = jnp.sum(shifted * shifted, axis=0, keepdims=True) * (1.0 / count)
    return shifted * lax.rsqrt(second + 1e-05) * gain


def layer_kernel(
    at_head,
    links,
    perm,
    lookup,
    peer_feats,
    near_list,
    rows_a,
    rows_b,
    feats,
    mask,
    vids,
    vtab,
    weights,
    wo,
    gains,
    out,
    table,
    far,
    q_t,
    q_rows,
    k_rows,
    v_t,
    far_w,
):
    del at_head
    nodes, width = feats.shape
    n_head = weights.shape[0]
    local = width // n_head
    heads = width // HEAD_DIM
    link_count = links.shape[0]
    n_virt = vtab.shape[0]
    f_rows = (weights.shape[1] - 3 * local) // 2

    def gathered(lo, count):
        return jnp.concatenate([weights[h, lo : lo + count, :] for h in range(n_head)], axis=0)

    wq_t = gathered(0, local)
    wk_t = gathered(local, local)
    wv_t = gathered(2 * local, local)
    w1_t = gathered(3 * local, f_rows)
    eye = (
        lax.broadcasted_iota(jnp.int32, (width, width), 0)
        == lax.broadcasted_iota(jnp.int32, (width, width), 1)
    ).astype(BF16)
    w2_t = dot_nt(eye, gathered(3 * local + f_rows, f_rows)).astype(BF16)
    wo_t = dot_nt(eye, wo[...]).astype(BF16)
    gain_cols = [
        jnp.transpose(jnp.broadcast_to(gains[g : g + 1, :], (width, width))) for g in (0, 1)
    ]
    far_w[...] = jnp.concatenate([wk_t, wv_t], axis=0)
    far_t = far_w[...]

    widen(peer_feats, table, 0, peer_feats.shape[0])
    widen(near_list, table, peer_feats.shape[0], near_list.shape[0])
    for e in range(link_count):
        gather_rows(nodes, lambda r, e=e: lookup[links[e, r]], table, far, e * nodes)
    gather_rows(nodes, lambda r: perm[0, 0, r], table, far, link_count * nodes)

    scale = HEAD_DIM ** (-0.5)
    own = feats[...]
    q_rows[...] = (dot_nt(own, wq_t).astype(BF16) * scale).astype(BF16)
    k_rows[...] = dot_nt(own, wk_t).astype(BF16)
    q_t[...] = (dot_nt(wq_t, own).astype(BF16) * scale).astype(F32)
    v_t[...] = dot_nt(wv_t, own).astype(BF16)
    vk = dot_nt(vtab[...], wk_t).astype(BF16)
    vv_t = dot_nt(wv_t, vtab[...]).astype(BF16)

    lane_head = lax.broadcasted_iota(jnp.int32, (BLOCK, width), 1) // HEAD_DIM
    sub_head = lax.broadcasted_iota(jnp.int32, (width, BLOCK), 0) // HEAD_DIM
    zero = jnp.zeros((), BF16)

    def by_head_rows(rows):
        lanes = lane_head[0 : rows.shape[0]]
        return jnp.concatenate([jnp.where(lanes == h, rows, zero) for h in range(heads)], axis=0)

    def by_head_cols(cols):
        subs = lax.broadcasted_iota(jnp.int32, cols.shape, 0) // HEAD_DIM
        return jnp.concatenate([jnp.where(subs == h, cols, zero) for h in range(heads)], axis=1)

    vk_heads = by_head_rows(vk)
    vv_heads = by_head_cols(vv_t)
    eyes = jnp.concatenate([eye] * heads, axis=0)
    diag = lax.broadcasted_iota(jnp.int32, (BLOCK, BLOCK), 0) == lax.broadcasted_iota(
        jnp.int32, (BLOCK, BLOCK), 1
    )

    def expand(per_head):
        return jnp.broadcast_to(
            per_head[:, None, :], (heads, HEAD_DIM, per_head.shape[-1])
        ).reshape(width, per_head.shape[-1])

    def step(b, carry):
        at = pl.multiple_of(b * BLOCK, BLOCK)
        here = pl.ds(at, BLOCK)
        feat = feats[here, :]
        k_heads = jnp.concatenate([by_head_rows(k_rows[here, :]), eyes], axis=1)
        allowed = (mask[here, :] > 0) | diag
        bias = jnp.where(allowed, 0.0, -1e30).astype(BF16)
        near = dot_nt(k_heads, jnp.concatenate([q_rows[here, :], bias], axis=1))
        near = near.reshape(heads, BLOCK, BLOCK)
        hub = dot_nt(vk_heads, q_rows[here, :]).reshape(heads, n_virt, BLOCK)
        mine = vids[0:1, here] == lax.broadcasted_iota(jnp.int32, (n_virt, BLOCK), 0)
        hub = jnp.where(mine[None], hub, -1e30)
        queries = q_t[:, here]
        far_scores = []
        far_values = []
        for e in range(link_count + 3):
            if e <= link_count:
                rows = far[pl.ds(pl.multiple_of(e * nodes + at, BLOCK), BLOCK), :].astype(BF16)
            else:
                rows = (rows_a if e == link_count + 1 else rows_b)[here, :]
            kv = dot_nt(far_t, rows).astype(BF16).astype(F32)
            prod = (kv[0:width] * queries).reshape(heads, HEAD_DIM, BLOCK)
            far_scores.append(jnp.sum(prod, axis=1))
            far_values.append(kv[width:])
        top = jnp.maximum(jnp.max(near, axis=1), jnp.max(hub, axis=1))
        for scored in far_scores:
            top = jnp.maximum(top, scored)
        near_exp = jnp.exp(near - top[:, None, :])
        hub_exp = jnp.exp(hub - top[:, None, :])
        total = jnp.sum(near_exp, axis=1) + jnp.sum(hub_exp, axis=1)
        mixed = dot_nn(
            by_head_cols(v_t[:, here]), near_exp.astype(BF16).reshape(heads * BLOCK, BLOCK)
        )
        mixed = mixed + dot_nn(vv_heads, hub_exp.astype(BF16).reshape(heads * n_virt, BLOCK))
        for scored, values in zip(far_scores, far_values):
            weight = jnp.exp(scored - top)
            total = total + weight
            mixed = mixed + expand(weight) * values
        attended = (mixed * expand(1.0 / total)).astype(BF16)
        residual = dot_nt(eye, feat) + dot_nn(wo_t, attended)
        hidden = layer_norm_cols(residual, gain_cols[0]).astype(BF16)
        inner = jax.nn.gelu(dot_nn(w1_t, hidden), approximate=True).astype(BF16)
        summed = hidden.astype(F32) + dot_nn(w2_t, inner)
        out[here, :] = jnp.transpose(layer_norm_cols(summed, gain_cols[1])).astype(BF16)
        return carry

    lax.fori_loop(0, nodes // BLOCK, step, 0)


def per_device(
    features,
    qkv_weight,
    out_weight,
    ffn_in,
    ffn_out,
    norm_gains,
    virtual_table,
    block_mask,
    halo_send,
    halo_links,
    expander_perm,
    virtual_ids,
):
    nodes, width = features.shape
    n_dom = lax.axis_size("dom")
    n_head = lax.axis_size("head")
    part = nodes // n_head
    halo = halo_send.shape[2]
    wqkv = jnp.transpose(qkv_weight, (1, 2, 0)).reshape(-1, width)
    w1 = ffn_in.T
    w_rows = wqkv.shape[0] + 2 * w1.shape[0]
    send = halo_send.reshape(2, halo)
    links = halo_links.T
    vids = virtual_ids.reshape(1, nodes)
    chunk = 512
    any_space = pl.BlockSpec(memory_space=pl.ANY)
    vmem = pl.BlockSpec(memory_space=pltpu.VMEM)
    smem = pl.BlockSpec(memory_space=pltpu.SMEM)
    dma = pltpu.SemaphoreType.DMA
    lists = halo // chunk
    pieces = part // chunk
    peer_feats, near_list, rows_a, rows_b, lookup, weights = pl.pallas_call(
        functools.partial(exchange_kernel, n_dom, n_head),
        name="exchange",
        out_shape=(
            jax.ShapeDtypeStruct((nodes, width), BF16),
            jax.ShapeDtypeStruct((halo, width), BF16),
            jax.ShapeDtypeStruct((part, width), BF16),
            jax.ShapeDtypeStruct((part, width), BF16),
            jax.ShapeDtypeStruct((2, halo), jnp.int32),
            jax.ShapeDtypeStruct((n_head, w_rows, width), BF16),
        ),
        in_specs=[vmem, smem, vmem, any_space, vmem, vmem, vmem],
        out_specs=(any_space, any_space, any_space, any_space, vmem, any_space),
        scratch_shapes=[
            pltpu.VMEM((nodes, width), F32),
            pltpu.VMEM((chunk, width), F32),
            pltpu.VMEM((lists + 2 * pieces, chunk, width), BF16),
            pltpu.VMEM((w_rows, width), BF16),
            pltpu.VMEM((2, halo), jnp.int32),
            pltpu.VMEM((2, part), jnp.int32),
            pltpu.SMEM((2, part), jnp.int32),
            dma((2,)),
            dma((2,)),
            dma((2,)),
            dma((2,)),
            dma((lists,)),
            dma((lists,)),
            dma((2 * pieces,)),
            dma((2 * pieces,)),
            dma((n_head - 1,)),
            dma((n_head,)),
            dma((3,)),
        ],
        compiler_params=pltpu.CompilerParams(
            collective_id=0, has_side_effects=True, vmem_limit_bytes=48 << 20
        ),
    )(features, send, send, expander_perm, wqkv, w1, ffn_out)

    head = lax.axis_index("head").astype(jnp.int32).reshape(1)
    grid_spec = pltpu.PrefetchScalarGridSpec(
        num_scalar_prefetch=1,
        grid=(1,),
        in_specs=[
            pl.BlockSpec((links.shape[0], part), lambda i, h: (0, h[0]), memory_space=pltpu.SMEM),
            pl.BlockSpec((1, 1, part), lambda i, h: (0, 0, h[0]), memory_space=pltpu.SMEM),
            smem,
            vmem,
            vmem,
            vmem,
            vmem,
            pl.BlockSpec((part, width), lambda i, h: (h[0], 0)),
            pl.BlockSpec((part, BLOCK), lambda i, h: (h[0], 0)),
            pl.BlockSpec((1, part), lambda i, h: (0, h[0])),
            vmem,
            vmem,
            vmem,
            vmem,
        ],
        out_specs=pl.BlockSpec((part, width), lambda i, h: (0, 0)),
        scratch_shapes=[
            pltpu.VMEM((nodes + halo, width), F32),
            pltpu.VMEM(((links.shape[0] + 1) * part, width), F32),
            pltpu.VMEM((width, part), F32),
            pltpu.VMEM((part, width), BF16),
            pltpu.VMEM((part, width), BF16),
            pltpu.VMEM((width, part), BF16),
            pltpu.VMEM((2 * width, width), BF16),
        ],
    )
    return pl.pallas_call(
        layer_kernel,
        name="layer",
        grid_spec=grid_spec,
        out_shape=jax.ShapeDtypeStruct((part, width), BF16),
        compiler_params=pltpu.CompilerParams(vmem_limit_bytes=48 << 20),
    )(
        head,
        links,
        expander_perm,
        lookup.reshape(2 * halo),
        peer_feats,
        near_list,
        rows_a,
        rows_b,
        features,
        block_mask,
        vids,
        virtual_table,
        weights,
        out_weight,
        norm_gains,
    )


def solution(mesh):
    return jax.shard_map(
        per_device,
        mesh=mesh,
        in_specs=(
            P("dom", None),
            P(None, None, "head"),
            P(),
            P(None, "head"),
            P("head", None),
            P(),
            P(),
            P("dom", None),
            P("dom", None, None),
            P("dom", None),
            P(None, "dom", None),
            P("dom"),
        ),
        out_specs=P(("dom", "head"), None),
        check_vma=False,
    )
```

time: 271 us -> 60.1 us (0.22)
  local copies, waits for them, and re-layouts: 154 us -> 10.2 us
  Pallas kernels: 0 us -> 49.2 us
  waiting for transfers between devices: 47.9 us -> 0 us
  other arithmetic: 33.8 us -> 0 us
  between operations: 14.1 us -> 0.04 us
  matrix products: 12.3 us -> 0 us
  starting transfers between devices: 8.49 us -> 0 us
    gather x9 -> x0, local copies, waits for them, and re-layouts: 127 us -> none  [pick_rows(): return jnp.take(table, indices, axis=0)]
    pallas_call x0 -> x2, Pallas kernels: none -> 49.2 us  [the longest x1 25.1 us: per_device(): pl.pallas_call(layer_kernel, name='layer', grid_spec=grid_spec, out_shape...]
    reduce_scatter x1 -> x0, waiting for transfers between devices: 24 us -> none  [per_device(): lax.psum_scatter(partial_out.astype(jnp.bfloat16), 'head', scatter_dimens...]
    all_gather x1 -> x0, waiting for transfers between devices: 23.9 us -> none  [per_device(): lax.all_gather(attended, 'head', axis=1, tiled=True)]
    dot_general x6 -> x0, matrix products: 12.3 us -> none  [the longest x1 3.59 us: attend(): jnp.einsum('bihd,bjhd->bihj', q_blocks, k_blocks, preferred_element_type=...]
    ppermute x5 -> x0, starting transfers between devices: 8.45 us -> none  [the longest x3 7.16 us: from_partner(): return lax.ppermute(block, axis, route)]
    slice x8 -> x0, local copies, waits for them, and re-layouts: 7.69 us -> none  [the longest x1 2.73 us: per_device(): paired[..., :local_width]]
    reduce_sum x6 -> x0, other arithmetic: 6.02 us -> none  [the longest x1 3.4 us: attend(): row_total = jnp.sum(near_exp, axis=-1, keepdims=True)]
  transfers between devices with their start and end apart: 7 -> 0, of which waited for: 2 -> 0; matrix products, arithmetic and copies ran while one was open for 55% -> 0% of each run, Pallas kernels for 0% -> 0%
where the time goes in v1:
time: 60.1 us; the launch traced here: 59.4 us
  Pallas kernels  49.2 us (82%)
  local copies, waits for them, and re-layouts  10.2 us (17%)
    pallas_call x1, Pallas kernels, per_device(): pl.pallas_call(layer_kernel, name='layer', grid_spec=grid_spec, out_shape...  25.1 us
    pallas_call x1, Pallas kernels, per_device(): pl.pallas_call(functools.partial(exchange_kernel, n_dom, n_head), name='e...  24.1 us
    unnamed x25, local copies, waits for them, and re-layouts  10.2 us

profile of v1, /device:TPU:0, one launch (start us, length us, event | category | flops | bytes accessed | tf_op | source)
XLA Modules:
  0.0 59.4 jit_solution(16714468163203464673)
XLA Ops:
  0.0 0.0 copy-start
  0.0 1.2 %copy-done = bf16[4096,128]{1,0:T(8,128)(2,1)S(1)} copy-done((bf16[4096,128]{1,0:T(8,128)(2,1)S(1)}, bf16[4096,128]{1,0:T(8,128)(2,1)}, u32[]{:S(2)}) %copy-start) | copy-done | bytes 1048600
  1.2 0.0 copy-start.2
  1.2 0.8 %copy-done.2 = s32[3,1,4096]{2,1,0:T(1,128)S(1)} copy-done((s32[3,1,4096]{2,1,0:T(1,128)S(1)}, s32[3,1,4096]{2,1,0:T(1,128)}, u32[]{:S(2)}) %copy-start.2) | copy-done | bytes 49176
  2.0 0.0 copy-start.4
  2.0 0.7 %copy-done.4 = s32[1,2,2048]{2,1,0:T(2,128)S(1)} copy-done((s32[1,2,2048]{2,1,0:T(2,128)S(1)}, s32[1,2,2048]{2,1,0:T(2,128)}, u32[]{:S(2)}) %copy-start.4) | copy-done | bytes 16408
  2.7 0.0 copy-start.6
  2.7 0.7 %copy-done.6 = bf16[128,3,32]{0,2,1:T(8,128)(2,1)S(1)} copy-done((bf16[128,3,32]{0,2,1:T(8,128)(2,1)S(1)}, bf16[128,3,32]{0,2,1:T(8,128)(2,1)}, u32[]{:S(2)}) %copy-start.6) | copy-done | bytes 24600
  3.5 0.0 copy-start.7
  3.5 0.7 %copy-done.7 = bf16[128,64]{0,1:T(8,128)(2,1)S(1)} copy-done((bf16[128,64]{0,1:T(8,128)(2,1)S(1)}, bf16[128,64]{0,1:T(8,128)(2,1)}, u32[]{:S(2)}) %copy-start.7) | copy-done | bytes 16408
  4.2 0.0 copy-start.8
  4.2 0.7 %copy-done.8 = bf16[64,128]{1,0:T(8,128)(2,1)S(1)} copy-done((bf16[64,128]{1,0:T(8,128)(2,1)S(1)}, bf16[64,128]{1,0:T(8,128)(2,1)}, u32[]{:S(2)}) %copy-start.8) | copy-done | bytes 16408
  4.9 24.1 %exchange.1 = (bf16[4096,128]{1,0:T(8,128)(2,1)S(1)}, bf16[2048,128]{1,0:T(8,128)(2,1)S(1)}, bf16[1024,128]{1,0:T(8,128)(2,1)S(1)}, bf16[1024,128]{1,0:T(8,128)(...) custom-call(bf16[4096,128]{1,0:T(8,128)(2,1)S(1)} %copy-done, s32[2,2048]{1,0:T(2,128)S(1)} %bitcast.11, ...), custom_call_target="tpu_custom_call" | custom-call | tf_op jit(solution)/shard_map/exchange/pallas_call | solution.py:383
  29.0 0.0 copy-start.1
  29.0 1.6 %copy-done.1 = s32[4096,128]{1,0:T(8,128)S(1)} copy-done((s32[4096,128]{1,0:T(8,128)S(1)}, s32[4096,128]{1,0:T(8,128)}, u32[]{:S(2)}) %copy-start.1) | copy-done | bytes 2097176
  30.6 0.0 copy-start.3
  30.6 0.8 %copy-done.3 = s32[4096,4]{0,1:T(4,128)S(1)} copy-done((s32[4096,4]{0,1:T(4,128)S(1)}, s32[4096,4]{0,1:T(4,128)}, u32[]{:S(2)}) %copy-start.3) | copy-done | bytes 65560
  31.4 0.0 copy-start.5
  31.5 0.8 %copy-done.5 = bf16[128,128]{1,0:T(8,128)(2,1)S(1)} copy-done((bf16[128,128]{1,0:T(8,128)(2,1)S(1)}, bf16[128,128]{1,0:T(8,128)(2,1)}, u32[]{:S(2)}) %copy-start.5) | copy-done | bytes 32792
  32.2 0.0 copy-start.9
  32.2 0.7 %copy-done.9 = s32[4096]{0:T(1024)S(1)} copy-done((s32[4096]{0:T(1024)S(1)}, s32[4096]{0:T(1024)}, u32[]{:S(2)}) %copy-start.9) | copy-done | bytes 16408
  32.9 0.0 copy-start.10
  32.9 0.7 %copy-done.10 = bf16[8,128]{1,0:T(8,128)(2,1)S(1)} copy-done((bf16[8,128]{1,0:T(8,128)(2,1)S(1)}, bf16[8,128]{1,0:T(8,128)(2,1)}, u32[]{:S(2)}) %copy-start.10) | copy-done | bytes 2072
  33.6 0.0 copy-start.11
  33.6 0.7 %copy-done.11 = f32[2,128]{1,0:T(2,128)S(1)} copy-done((f32[2,128]{1,0:T(2,128)S(1)}, f32[2,128]{1,0:T(2,128)}, u32[]{:S(2)}) %copy-start.11) | copy-done | bytes 1048
  34.3 25.1 %layer.1 = bf16[1024,128]{1,0:T(8,128)(2,1)} custom-call(s32[1]{0:T(128)} %bitcast.at_head, s32[4,4096]{1,0:T(4,128)S(1)} %bitcast.10, s32[3,1,4096]{2,1,0:T(1,128)S(1)} %copy-done.2, s32[4096]{0:T(1024)S(1)} %bitcast.13, bf16[4096,128]{1,0:T(8,128)(2,1)S(1)} %get-tuple-element.12.peer_feats, bf16[2048,128]{1,0:T(8,128)(2,1)S(1)} %get-tuple-element.13.near_list, ...), custom_call_target="tpu_custom_call" | custom-call | tf_op jit(solution)/shard_map/layer/pallas_call | solution.py:452
  (1 shorter events, 0.0 us)
Async XLA Ops:
  0.0 1.2 %copy-start = (bf16[4096,128]{1,0:T(8,128)(2,1)S(1)}, bf16[4096,128]{1,0:T(8,128)(2,1)}, u32[]{:S(2)}) copy-start(bf16[4096,128]{1,0:T(8,128)(2,1)} %feats.3) | copy-start | bytes 3145732
  1.2 0.8 %copy-start.2 = (s32[3,1,4096]{2,1,0:T(1,128)S(1)}, s32[3,1,4096]{2,1,0:T(1,128)}, u32[]{:S(2)}) copy-start(s32[3,1,4096]{2,1,0:T(1,128)} %perm.3) | copy-start | bytes 147460
  2.0 0.7 %copy-start.4 = (s32[1,2,2048]{2,1,0:T(2,128)S(1)}, s32[1,2,2048]{2,1,0:T(2,128)}, u32[]{:S(2)}) copy-start(s32[1,2,2048]{2,1,0:T(2,128)} %param.20) | copy-start | bytes 49156
  2.7 0.7 %copy-start.6 = (bf16[128,3,32]{0,2,1:T(8,128)(2,1)S(1)}, bf16[128,3,32]{0,2,1:T(8,128)(2,1)}, u32[]{:S(2)}) copy-start(bf16[128,3,32]{0,2,1:T(8,128)(2,1)} %param.13) | copy-start | bytes 73732
  3.5 0.7 %copy-start.7 = (bf16[128,64]{0,1:T(8,128)(2,1)S(1)}, bf16[128,64]{0,1:T(8,128)(2,1)}, u32[]{:S(2)}) copy-start(bf16[128,64]{0,1:T(8,128)(2,1)} %param.15) | copy-start | bytes 49156
  4.2 0.7 %copy-start.8 = (bf16[64,128]{1,0:T(8,128)(2,1)S(1)}, bf16[64,128]{1,0:T(8,128)(2,1)}, u32[]{:S(2)}) copy-start(bf16[64,128]{1,0:T(8,128)(2,1)} %w2.1) | copy-start | bytes 49156
  29.0 1.6 %copy-start.1 = (s32[4096,128]{1,0:T(8,128)S(1)}, s32[4096,128]{1,0:T(8,128)}, u32[]{:S(2)}) copy-start(s32[4096,128]{1,0:T(8,128)} %mask.1) | copy-start | bytes 6291460
  30.6 0.8 %copy-start.3 = (s32[4096,4]{0,1:T(4,128)S(1)}, s32[4096,4]{0,1:T(4,128)}, u32[]{:S(2)}) copy-start(s32[4096,4]{0,1:T(4,128)} %param.21) | copy-start | bytes 196612
  31.4 0.8 %copy-start.5 = (bf16[128,128]{1,0:T(8,128)(2,1)S(1)}, bf16[128,128]{1,0:T(8,128)(2,1)}, u32[]{:S(2)}) copy-start(bf16[128,128]{1,0:T(8,128)(2,1)} %wo.1) | copy-start | bytes 98308
  32.2 0.7 %copy-start.9 = (s32[4096]{0:T(1024)S(1)}, s32[4096]{0:T(1024)}, u32[]{:S(2)}) copy-start(s32[4096]{0:T(1024)} %param.23) | copy-start | bytes 49156
  32.9 0.7 %copy-start.10 = (bf16[8,128]{1,0:T(8,128)(2,1)S(1)}, bf16[8,128]{1,0:T(8,128)(2,1)}, u32[]{:S(2)}) copy-start(bf16[8,128]{1,0:T(8,128)(2,1)} %vtab.1) | copy-start | bytes 6148
  33.6 0.7 %copy-start.11 = (f32[2,128]{1,0:T(2,128)S(1)}, f32[2,128]{1,0:T(2,128)}, u32[]{:S(2)}) copy-start(f32[2,128]{1,0:T(2,128)} %gains.1) | copy-start | bytes 3076

commit v2 on v0

v2 whole, which is shorter than its diff:
```python
import functools

import jax
import jax.numpy as jnp
from jax import lax
from jax.experimental import pallas as pl
from jax.experimental.pallas import tpu as pltpu
from jax.sharding import PartitionSpec as P

HEAD_DIM = 16
BLOCK = 128
ROWS = 64
CHUNK = 512
MESH = pl.DeviceIdType.MESH
F32 = jnp.float32
BF16 = jnp.bfloat16
NEG = -1e30


def dot_nt(a, b):
    return lax.dot_general(a, b, (((1,), (1,)), ((), ())), preferred_element_type=F32)


def dot_nn(a, b):
    return jnp.dot(a, b, preferred_element_type=F32)


def iota(shape, dim):
    return lax.broadcasted_iota(jnp.int32, shape, dim)


def gather_rows(count, index, index_base, table, out, out_base):
    def step(i, carry):
        base = pl.multiple_of(i * ROWS, ROWS)
        for u in range(ROWS):
            row = index[index_base + base + u]
            out[pl.ds(out_base + base + u, 1), :] = table[pl.ds(row, 1), :]
        return carry

    lax.fori_loop(0, count // ROWS, step, 0)


def widen(source, source_base, out, out_base, rows):
    def step(i, carry):
        at = pl.multiple_of(i * 256, 256)
        out[pl.ds(out_base + at, 256), :] = source[pl.ds(source_base + at, 256), :].astype(F32)
        return carry

    lax.fori_loop(0, rows // 256, step, 0)


def layer_norm_cols(values, gain):
    count = values.shape[0]
    center = jnp.sum(values, axis=0, keepdims=True) * (1.0 / count)
    shifted = values - center
    second = jnp.sum(shifted * shifted, axis=0, keepdims=True) * (1.0 / count)
    return shifted * lax.rsqrt(second + 1e-05) * gain


def prepare(weights, wo, gains, vtab, own, wq_p, wkv_p, w1_t, w2_t, wo_t, gain_cols, q_rows, k_rows, q_t, v_t, vk_h, vv_h):
    n_head, _, width = weights.shape
    local = width // n_head
    heads = width // HEAD_DIM
    f_rows = (weights.shape[1] - 3 * local) // 2

    def whole(lo, count):
        return jnp.concatenate([weights[h, lo : lo + count, :] for h in range(n_head)], axis=0)

    row, col = iota((width, width), 0), iota((width, width), 1)
    order = (col == lax.rem(row, heads) * HEAD_DIM + row // heads).astype(BF16)
    eye = (row == col).astype(BF16)
    scale = HEAD_DIM ** (-0.5)
    wq = (dot_nn(order, whole(0, local)) * scale).astype(BF16)
    wk = dot_nn(order, whole(local, local)).astype(BF16)
    wv = dot_nn(order, whole(2 * local, local)).astype(BF16)
    wkv_p[0:width, :] = wk
    wkv_p[width : 2 * width, :] = wv
    w1_t[...] = whole(3 * local, f_rows)
    w2_t[...] = dot_nt(eye, whole(3 * local + f_rows, f_rows)).astype(BF16)
    wo_t[...] = dot_nt(eye, dot_nn(order, wo[...]).astype(BF16)).astype(BF16)
    for g in (0, 1):
        gain_cols[g] = jnp.transpose(jnp.broadcast_to(gains[g : g + 1, :], (width, width)))
    q_rows[...] = dot_nt(own, wq).astype(BF16)
    k_rows[...] = dot_nt(own, wk).astype(BF16)
    q_t[...] = dot_nt(wq, own).astype(BF16).astype(F32)
    v_t[...] = dot_nt(wv, own).astype(BF16)
    vk = dot_nt(vtab, wk).astype(BF16)
    vv = dot_nt(wv, vtab).astype(BF16)
    zero = jnp.zeros((), BF16)
    vk_h[...] = jnp.concatenate(
        [jnp.where(lax.rem(iota(vk.shape, 1), heads) == h, vk, zero) for h in range(heads)], axis=0
    )
    vv_h[...] = jnp.concatenate(
        [jnp.where(lax.rem(iota(vv.shape, 0), heads) == h, vv, zero) for h in range(heads)], axis=1
    )


def near_block(b, mask, vids, q_rows, k_rows, v_t, vk_h, vv_h, near_out, near_top, near_sum, fill=None):
    width = q_rows.shape[1]
    heads = width // HEAD_DIM
    n_virt = vk_h.shape[0] // heads
    here = pl.ds(b * BLOCK, BLOCK) if isinstance(b, int) else pl.ds(pl.multiple_of(b * BLOCK, BLOCK), BLOCK)
    row, col = iota((BLOCK, BLOCK), 0), iota((BLOCK, BLOCK), 1)
    eye = (row == col).astype(BF16)
    bias = jnp.where((mask[here, :] > 0) | (row == col), 0.0, NEG).astype(BF16)
    bias_t = dot_nt(eye, bias)
    zero = jnp.zeros((), BF16)
    keys, queries, values = k_rows[here, :], q_rows[here, :], v_t[:, here]
    lane_h, sub_h = lax.rem(iota((BLOCK, width), 1), heads), lax.rem(iota((width, BLOCK), 0), heads)
    scores = dot_nt(
        jnp.concatenate([jnp.where(lane_h == h, keys, zero) for h in range(heads)], axis=0), queries
    )
    hub = dot_nt(vk_h[...], queries)
    mine = vids[0:1, here] == iota((n_virt, BLOCK), 0)
    tops, sums, near_p, hub_p = [], [], [], []
    for h in range(heads):
        near = scores[h * BLOCK : (h + 1) * BLOCK] + bias_t
        virt = jnp.where(mine, hub[h * n_virt : (h + 1) * n_virt], NEG)
        top = jnp.maximum(
            jnp.max(near, axis=0, keepdims=True), jnp.max(virt, axis=0, keepdims=True)
        )
        near = jnp.exp(near - top)
        virt = jnp.exp(virt - top)
        tops.append(top)
        sums.append(jnp.sum(near, axis=0, keepdims=True) + jnp.sum(virt, axis=0, keepdims=True))
        near_p.append(near.astype(BF16))
        hub_p.append(virt)
        if fill is not None:
            fill(h)
    near_top[:, here] = jnp.concatenate(tops, axis=0)
    near_sum[:, here] = jnp.concatenate(sums, axis=0)
    by_head = jnp.concatenate([jnp.where(sub_h == h, values, zero) for h in range(heads)], axis=1)
    near_out[:, here] = dot_nn(by_head, jnp.concatenate(near_p, axis=0)) + dot_nn(
        vv_h[...], jnp.concatenate(hub_p, axis=0).astype(BF16)
    )


def far_chunk(c, size, row_refs, wkv_p, q_t, near_out, near_top, near_sum, attended):
    width = q_t.shape[0]
    heads = width // HEAD_DIM
    at = c * size if isinstance(c, int) else pl.multiple_of(c * size, size)
    here = pl.ds(at, size)
    split = (HEAD_DIM, heads, size)
    queries = q_t[:, here].reshape(split)
    wkv = wkv_p[...]
    scored, values = [], []
    for ref, first in row_refs:
        rows = ref[pl.ds(first + at, size), :].astype(BF16)
        kv = dot_nt(wkv, rows)
        keys = kv[0:width].astype(BF16).astype(F32).reshape(split)
        scored.append(jnp.sum(keys * queries, axis=0))
        values.append(kv[width:].reshape(split))
    top = near_top[:, here]
    for s in scored:
        top = jnp.maximum(top, s)
    shrink = jnp.exp(near_top[:, here] - top)
    total = near_sum[:, here] * shrink
    mixed = near_out[:, here].reshape(split) * shrink[None]
    for s, v in zip(scored, values):
        weight = jnp.exp(s - top)
        total = total + weight
        mixed = mixed + v * weight[None]
    attended[:, here] = (mixed * (1.0 / total)[None]).reshape(width, size).astype(BF16)


def ffn_chunk(c, size, own, attended, wo_t, w1_t, w2_t, gain_cols, out):
    width = attended.shape[0]
    at = c * size if isinstance(c, int) else pl.multiple_of(c * size, size)
    here = pl.ds(at, size)
    eye = (iota((width, width), 0) == iota((width, width), 1)).astype(BF16)
    gain = [jnp.concatenate([gain_cols[g]] * (size // width), axis=1) for g in (0, 1)]
    residual = dot_nt(eye, own(here)) + dot_nn(wo_t[...], attended[:, here])
    hidden = layer_norm_cols(residual, gain[0]).astype(BF16)
    inner = jax.nn.gelu(dot_nn(w1_t[...], hidden), approximate=True).astype(BF16)
    summed = layer_norm_cols(hidden.astype(F32) + dot_nn(w2_t[...], inner), gain[1])
    for k in range(size // width):
        out[pl.ds(at + k * width, width), :] = jnp.transpose(
            summed[:, k * width : (k + 1) * width]
        ).astype(BF16)


def layer_kernel(
    n_dom,
    n_head,
    feats_in,
    wqkv_in,
    wo_in,
    w1_in,
    w2_in,
    gains_in,
    vtab_in,
    mask_in,
    send_in,
    links_in,
    perm_in,
    vids_in,
    out,
    feats,
    table,
    staged,
    packed,
    weights,
    wo,
    gains,
    vtab,
    mask,
    vids,
    send_first,
    send_second,
    links,
    request,
    wanted,
    lists,
    matched,
    far,
    wq_p,
    wkv_p,
    w1_t,
    w2_t,
    wo_t,
    gain_cols,
    q_rows,
    k_rows,
    q_t,
    v_t,
    vk_h,
    vv_h,
    near_out,
    near_top,
    near_sum,
    attended,
    local_sems,
    req_send,
    req_recv,
    list_send,
    list_recv,
    rows_send,
    rows_recv,
    w_send,
    w_recv,
):
    nodes = feats.shape[0]
    part = out.shape[0]
    halo = lists.shape[0] // 2
    chunk = staged.shape[0]
    link_count = links_in.shape[0]
    dom = lax.axis_index("dom")
    head = lax.axis_index("head")
    core = lax.rem(dom, 2)
    peer = dom + 1 - 2 * core
    side = lax.rem(dom + 2 * core - 1 + n_dom, n_dom)
    levels = n_dom.bit_length() - 1
    mine = pl.ds(pl.multiple_of(head * part, part), part)

    def flipped(stride):
        bit = lax.rem(dom // (1 << stride), 2)
        return dom + (1 - 2 * bit) * (1 << stride)

    partners = [flipped(m * (levels - 1) // 2) for m in range(3)]
    others = [lax.rem(head + k, n_head) for k in range(1, n_head)]

    barrier = pltpu.get_barrier_semaphore()
    for dev in [side] + partners:
        pl.semaphore_signal(barrier, inc=1, device_id={"dom": dev}, device_id_type=MESH)
    for dev in others:
        pl.semaphore_signal(barrier, inc=1, device_id={"head": dev}, device_id_type=MESH)

    def fetch(k, src, dst):
        copy = pltpu.make_async_copy(src, dst, local_sems.at[k])
        copy.start()
        return copy

    q_rows_in, f_rows = wqkv_in.shape[0], w1_in.shape[0]
    got_feats = fetch(0, feats_in, feats)
    got_first = fetch(1, send_in.at[0, core], send_first)
    got_second = fetch(2, send_in.at[0, 1 - core], send_second)
    got_weights = [
        fetch(3, wqkv_in, weights.at[head, pl.ds(0, q_rows_in)]),
        fetch(4, w1_in, weights.at[head, pl.ds(q_rows_in, f_rows)]),
        fetch(5, w2_in, weights.at[head, pl.ds(q_rows_in + f_rows, f_rows)]),
    ]
    got_rest = [
        fetch(6, wo_in, wo),
        fetch(7, gains_in, gains),
        fetch(8, vtab_in, vtab),
        fetch(9, mask_in.at[mine], mask),
        fetch(10, vids_in.at[:, mine], vids),
    ]
    got_links = [
        fetch(11 + e, links_in.at[e, mine], links.at[pl.ds(e * part, part)]) for e in range(link_count)
    ]

    def remote(src, dst, send, recv, device):
        return pltpu.make_async_remote_copy(
            src_ref=src, dst_ref=dst, send_sem=send, recv_sem=recv, device_id=device, device_id_type=MESH
        )

    pl.semaphore_wait(barrier, 4 + len(others))
    requests = []
    for m in range(3):
        copy = remote(
            perm_in.at[m, 0, mine], request.at[pl.ds(m * part, part)], req_send.at[m], req_recv.at[m], {"dom": partners[m]}
        )
        copy.start()
        requests.append(copy)
    for copy in got_weights:
        copy.wait()
    w_copies = []
    for k, dev in enumerate(others):
        copy = remote(weights.at[head], weights.at[head], w_send.at[k], w_recv.at[head], {"head": dev})
        copy.start()
        w_copies.append(copy)

    got_feats.wait()
    widen(feats, 0, table, 0, nodes)

    sent = []

    def send_chunk(index, at, dst, send, recv, device):
        slot = len(sent)
        gather_rows(chunk, index, at, table, staged, 0)
        packed[slot] = staged[...].astype(BF16)
        copy = remote(packed.at[slot], dst, send, recv, device)
        copy.start()
        sent.append(copy)

    count = halo // chunk
    for k, (got, index, row, dev) in enumerate(
        ((got_first, send_first, core, side), (got_second, send_second, 1 - core, peer))
    ):
        got.wait()
        for i in range(count):
            at = pl.multiple_of((1 - row) * halo + i * chunk, chunk)
            s = k * count + i
            send_chunk(
                index, i * chunk, lists.at[pl.ds(at, chunk)], list_send.at[s], list_recv.at[s], {"dom": dev}
            )
    list_copies = list(sent)

    for copy in requests:
        copy.wait_recv()
    got_wanted = [
        fetch(11 + link_count + m, request.at[pl.ds(m * part, part)], wanted.at[pl.ds(m * part, part)]) for m in range(3)
    ]
    pieces = part // chunk
    for m in (1, 2, 0):
        got_wanted[m].wait()
        for i in range(pieces):
            s = m * pieces + i
            send_chunk(
                wanted,
                m * part + i * chunk,
                matched.at[m, pl.ds(i * chunk, chunk)],
                rows_send.at[s],
                rows_recv.at[s],
                {"dom": partners[m]},
            )

    for dev in others:
        remote(weights.at[head], weights.at[dev], w_send.at[0], w_recv.at[dev], {"head": dev}).wait_recv()
    for copy in got_rest:
        copy.wait()
    prepare(
        weights, wo, gains, vtab[...], feats[mine, :], wq_p, wkv_p, w1_t, w2_t, wo_t, gain_cols,
        q_rows, k_rows, q_t, v_t, vk_h, vv_h,
    )
    for b in range(part // BLOCK):
        near_block(b, mask, vids, q_rows, k_rows, v_t, vk_h, vv_h, near_out, near_top, near_sum)

    for copy in list_copies:
        copy.wait_recv()
    widen(lists, 0, table, 0, 2 * halo)
    for copy in got_links:
        copy.wait()
    gather_rows(link_count * part, links, 0, table, far, 0)

    for copy in sent[len(list_copies) :]:
        copy.wait_recv()
    row_refs = [(far, e * part) for e in range(link_count)] + [(matched.at[m], 0) for m in range(3)]
    for c in range(part // 256):
        far_chunk(c, 256, row_refs, wkv_p, q_t, near_out, near_top, near_sum, attended)
    own_base = pl.multiple_of(head * part, part)
    ffn_chunk(
        0,
        part,
        lambda here: feats[pl.ds(own_base + here.start, here.size), :],
        attended,
        wo_t,
        w1_t,
        w2_t,
        gain_cols,
        out,
    )
    for copy in requests + w_copies + sent:
        copy.wait_send()


def per_device(
    features,
    qkv_weight,
    out_weight,
    ffn_in,
    ffn_out,
    norm_gains,
    virtual_table,
    block_mask,
    halo_send,
    halo_links,
    expander_perm,
    virtual_ids,
):
    nodes, width = features.shape
    n_dom = lax.axis_size("dom")
    n_head = lax.axis_size("head")
    part = nodes // n_head
    halo = halo_send.shape[2]
    heads = width // HEAD_DIM
    n_virt = virtual_table.shape[0]
    wqkv = jnp.transpose(qkv_weight, (1, 2, 0)).reshape(-1, width)
    w1 = ffn_in.T
    w_rows = wqkv.shape[0] + 2 * w1.shape[0]
    hidden = n_head * w1.shape[0]
    links = halo_links.T
    link_count = links.shape[0]
    vids = virtual_ids.reshape(1, nodes)
    chunk = CHUNK
    lists = 2 * halo // chunk
    pieces = 3 * part // chunk
    i32 = jnp.int32
    dma = pltpu.SemaphoreType.DMA
    return pl.pallas_call(
        functools.partial(layer_kernel, n_dom, n_head),
        name="layer",
        out_shape=jax.ShapeDtypeStruct((part, width), BF16),
        in_specs=[pl.BlockSpec(memory_space=pl.ANY)] * 12,
        out_specs=pl.BlockSpec(memory_space=pltpu.VMEM),
        scratch_shapes=[
            pltpu.VMEM((nodes, width), BF16),
            pltpu.VMEM((nodes, width), F32),
            pltpu.VMEM((chunk, width), F32),
            pltpu.VMEM((lists + pieces, chunk, width), BF16),
            pltpu.VMEM((n_head, w_rows, width), BF16),
            pltpu.VMEM((width, width), BF16),
            pltpu.VMEM((2, width), F32),
            pltpu.VMEM((n_virt, width), BF16),
            pltpu.VMEM((part, BLOCK), i32),
            pltpu.VMEM((1, part), i32),
            pltpu.SMEM((halo,), i32),
            pltpu.SMEM((halo,), i32),
            pltpu.SMEM((link_count * part,), i32),
            pltpu.VMEM((3 * part,), i32),
            pltpu.SMEM((3 * part,), i32),
            pltpu.VMEM((2 * halo, width), BF16),
            pltpu.VMEM((3, part, width), BF16),
            pltpu.VMEM((link_count * part, width), F32),
            pltpu.VMEM((width, width), BF16),
            pltpu.VMEM((2 * width, width), BF16),
            pltpu.VMEM((hidden, width), BF16),
            pltpu.VMEM((width, hidden), BF16),
            pltpu.VMEM((width, width), BF16),
            pltpu.VMEM((2, width, width), F32),
            pltpu.VMEM((part, width), BF16),
            pltpu.VMEM((part, width), BF16),
            pltpu.VMEM((width, part), F32),
            pltpu.VMEM((width, part), BF16),
            pltpu.VMEM((heads * n_virt, width), BF16),
            pltpu.VMEM((width, heads * n_virt), BF16),
            pltpu.VMEM((width, part), F32),
            pltpu.VMEM((heads, part), F32),
            pltpu.VMEM((heads, part), F32),
            pltpu.VMEM((width, part), BF16),
            dma((14 + link_count,)),
            dma((3,)),
            dma((3,)),
            dma((lists,)),
            dma((lists,)),
            dma((pieces,)),
            dma((pieces,)),
            dma((n_head - 1,)),
            dma((n_head,)),
        ],
        compiler_params=pltpu.CompilerParams(
            collective_id=0, has_side_effects=True, vmem_limit_bytes=60 << 20
        ),
    )(
        features,
        wqkv,
        out_weight,
        w1,
        ffn_out,
        norm_gains,
        virtual_table,
        block_mask,
        halo_send,
        links,
        expander_perm,
        vids,
    )


def solution(mesh):
    return jax.shard_map(
        per_device,
        mesh=mesh,
        in_specs=(
            P("dom", None),
            P(None, None, "head"),
            P(),
            P(None, "head"),
            P("head", None),
            P(),
            P(),
            P("dom", None),
            P("dom", None, None),
            P("dom", None),
            P(None, "dom", None),
            P("dom"),
        ),
        out_specs=P(("dom", "head"), None),
        check_vma=False,
    )
```

time: 271 us -> 28.1 us (0.10)
  the two profiles are of different devices: /device:TPU:0 before, /device:TPU:1 now
where the time goes in v2:
time: 28.1 us; the launch traced here: 28 us
  Pallas kernels  26.3 us (94%)
  local copies, waits for them, and re-layouts  1.67 us (6%)
    pallas_call x1, Pallas kernels, per_device(): pl.pallas_call(functools.partial(layer_kernel, n_dom, n_head), name='laye...  26.3 us
    unnamed x1, local copies, waits for them, and re-layouts  1.67 us

profile of v2, /device:TPU:1, one launch (start us, length us, event | category | flops | bytes accessed | tf_op | source)
XLA Modules:
  0.0 28.0 jit_solution(14046328975347640923)
XLA Ops:
  0.0 26.3 %layer.1 = bf16[1024,128]{1,0:T(8,128)(2,1)} custom-call(bf16[4096,128]{1,0:T(8,128)(2,1)} %feats_in.1, bf16[96,128]{1,0:T(8,128)(2,1)} %bitcast.7, bf16[128,128]{1,0:T(8,128)(2,1)} %wo_in.1, bf16[64,128]{1,0:T(8,128)(2,1)} %bitcast.8, bf16[64,128]{1,0:T(8,128)(2,1)} %w2_in.1, f32[2,128]{1,0:T(2,128)} %gains_in.1, bf16[8,128]{1,0:T(8,128)(2,1)} %vtab_in.1, ...), custom_call_target="tpu_custom_call" | custom-call | tf_op jit(solution)/shard_map/layer/pallas_call | solution.py:431
  26.3 1.7 %copy.14 = bf16[1024,128]{1,0:T(8,128)(2,1)} copy(bf16[1024,128]{1,0:T(8,128)(2,1)} %layer.1) | data formatting | bytes 524288

commit v3 on v2

--- a/solution.py
+++ b/solution.py
@@ -9,7 +9,6 @@
 
 HEAD_DIM = 16
 BLOCK = 128
-ROWS = 64
 CHUNK = 512
 MESH = pl.DeviceIdType.MESH
 F32 = jnp.float32
@@ -29,15 +28,9 @@
     return lax.broadcasted_iota(jnp.int32, shape, dim)
 
 
-def gather_rows(count, index, index_base, table, out, out_base):
-    def step(i, carry):
-        base = pl.multiple_of(i * ROWS, ROWS)
-        for u in range(ROWS):
-            row = index[index_base + base + u]
-            out[pl.ds(out_base + base + u, 1), :] = table[pl.ds(row, 1), :]
-        return carry
-
-    lax.fori_loop(0, count // ROWS, step, 0)
+def gather_rows(count, index, first, table, out, out_first):
+    for u in range(count):
+        out[out_first + u : out_first + u + 1, :] = table[pl.ds(index[first + u], 1), :]
 
 
 def widen(source, source_base, out, out_base, rows):
@@ -95,7 +88,7 @@
     )
 
 
-def near_block(b, mask, vids, q_rows, k_rows, v_t, vk_h, vv_h, near_out, near_top, near_sum, fill=None):
+def near_block(b, mask, vids, q_rows, k_rows, v_t, vk_h, vv_h, near_out, near_top, near_sum):
     width = q_rows.shape[1]
     heads = width // HEAD_DIM
     n_virt = vk_h.shape[0] // heads
@@ -108,13 +101,13 @@
     keys, queries, values = k_rows[here, :], q_rows[here, :], v_t[:, here]
     lane_h, sub_h = lax.rem(iota((BLOCK, width), 1), heads), lax.rem(iota((width, BLOCK), 0), heads)
     scores = dot_nt(
-        jnp.concatenate([jnp.where(lane_h == h, keys, zero) for h in range(heads)], axis=0), queries
+        keys, jnp.concatenate([jnp.where(lane_h == h, queries, zero) for h in range(heads)], axis=0)
     )
     hub = dot_nt(vk_h[...], queries)
     mine = vids[0:1, here] == iota((n_virt, BLOCK), 0)
     tops, sums, near_p, hub_p = [], [], [], []
     for h in range(heads):
-        near = scores[h * BLOCK : (h + 1) * BLOCK] + bias_t
+        near = scores[:, h * BLOCK : (h + 1) * BLOCK] + bias_t
         virt = jnp.where(mine, hub[h * n_virt : (h + 1) * n_virt], NEG)
         top = jnp.maximum(
             jnp.max(near, axis=0, keepdims=True), jnp.max(virt, axis=0, keepdims=True)
@@ -125,8 +118,6 @@
         sums.append(jnp.sum(near, axis=0, keepdims=True) + jnp.sum(virt, axis=0, keepdims=True))
         near_p.append(near.astype(BF16))
         hub_p.append(virt)
-        if fill is not None:
-            fill(h)
     near_top[:, here] = jnp.concatenate(tops, axis=0)
     near_sum[:, here] = jnp.concatenate(sums, axis=0)
     by_head = jnp.concatenate([jnp.where(sub_h == h, values, zero) for h in range(heads)], axis=1)
@@ -208,7 +199,6 @@
     send_first,
     send_second,
     links,
-    request,
     wanted,
     lists,
     matched,
@@ -238,6 +228,8 @@
     rows_recv,
     w_send,
     w_recv,
+    pass_send,
+    pass_recv,
 ):
     nodes = feats.shape[0]
     part = out.shape[0]
@@ -272,7 +264,8 @@
 
     q_rows_in, f_rows = wqkv_in.shape[0], w1_in.shape[0]
     got_feats = fetch(0, feats_in, feats)
-    got_first = fetch(1, send_in.at[0, core], send_first)
+    share = send_first.shape[0]
+    got_first = fetch(1, send_in.at[0, core, pl.ds(pl.multiple_of(head * share, share), share)], send_first)
     got_second = fetch(2, send_in.at[0, 1 - core], send_second)
     got_weights = [
         fetch(3, wqkv_in, weights.at[head, pl.ds(0, q_rows_in)]),
@@ -299,7 +292,7 @@
     requests = []
     for m in range(3):
         copy = remote(
-            perm_in.at[m, 0, mine], request.at[pl.ds(m * part, part)], req_send.at[m], req_recv.at[m], {"dom": partners[m]}
+            perm_in.at[m, 0, mine], wanted.at[pl.ds(m * part, part)], req_send.at[m], req_recv.at[m], {"dom": partners[m]}
         )
         copy.start()
         requests.append(copy)
@@ -324,27 +317,37 @@
         copy.start()
         sent.append(copy)
 
+    def shared(base, h):
+        return lists.at[pl.ds(pl.multiple_of(base * halo + h * share, share), share)]
+
+    got_first.wait()
+    send_chunk(send_first, 0, shared(1 - core, head), list_send.at[0], list_recv.at[0], {"dom": side})
+    got_second.wait()
     count = halo // chunk
-    for k, (got, index, row, dev) in enumerate(
-        ((got_first, send_first, core, side), (got_second, send_second, 1 - core, peer))
-    ):
-        got.wait()
-        for i in range(count):
-            at = pl.multiple_of((1 - row) * halo + i * chunk, chunk)
-            s = k * count + i
-            send_chunk(
-                index, i * chunk, lists.at[pl.ds(at, chunk)], list_send.at[s], list_recv.at[s], {"dom": dev}
-            )
+    for i in range(count):
+        at = pl.multiple_of(core * halo + i * chunk, chunk)
+        send_chunk(
+            send_second,
+            i * chunk,
+            lists.at[pl.ds(at, chunk)],
+            list_send.at[1 + i],
+            list_recv.at[1 + i],
+            {"dom": peer},
+        )
     list_copies = list(sent)
 
-    for copy in requests:
-        copy.wait_recv()
-    got_wanted = [
-        fetch(11 + link_count + m, request.at[pl.ds(m * part, part)], wanted.at[pl.ds(m * part, part)]) for m in range(3)
-    ]
     pieces = part // chunk
+    passed = []
     for m in (1, 2, 0):
-        got_wanted[m].wait()
+        if m == 0:
+            list_copies[0].wait_recv()
+            for k, dev in enumerate(others):
+                copy = remote(
+                    shared(core, head), shared(core, head), pass_send.at[k], pass_recv.at[head], {"head": dev}
+                )
+                copy.start()
+                passed.append(copy)
+        requests[m].wait_recv()
         for i in range(pieces):
             s = m * pieces + i
             send_chunk(
@@ -367,7 +370,11 @@
     for b in range(part // BLOCK):
         near_block(b, mask, vids, q_rows, k_rows, v_t, vk_h, vv_h, near_out, near_top, near_sum)
 
-    for copy in list_copies:
+    for dev in others:
+        remote(
+            shared(core, head), shared(core, dev), pass_send.at[0], pass_recv.at[dev], {"head": dev}
+        ).wait_recv()
+    for copy in list_copies[1:]:
         copy.wait_recv()
     widen(lists, 0, table, 0, 2 * halo)
     for copy in got_links:
@@ -391,7 +398,7 @@
         gain_cols,
         out,
     )
-    for copy in requests + w_copies + sent:
+    for copy in requests + w_copies + sent + passed:
         copy.wait_send()
 
 
@@ -424,7 +431,8 @@
     link_count = links.shape[0]
     vids = virtual_ids.reshape(1, nodes)
     chunk = CHUNK
-    lists = 2 * halo // chunk
+    share = halo // n_head
+    lists = 1 + halo // chunk
     pieces = 3 * part // chunk
     i32 = jnp.int32
     dma = pltpu.SemaphoreType.DMA
@@ -445,10 +453,9 @@
             pltpu.VMEM((n_virt, width), BF16),
             pltpu.VMEM((part, BLOCK), i32),
             pltpu.VMEM((1, part), i32),
-            pltpu.SMEM((halo,), i32),
+            pltpu.SMEM((share,), i32),
             pltpu.SMEM((halo,), i32),
             pltpu.SMEM((link_count * part,), i32),
-            pltpu.VMEM((3 * part,), i32),
             pltpu.SMEM((3 * part,), i32),
             pltpu.VMEM((2 * halo, width), BF16),
             pltpu.VMEM((3, part, width), BF16),
@@ -469,13 +476,15 @@
             pltpu.VMEM((heads, part), F32),
             pltpu.VMEM((heads, part), F32),
             pltpu.VMEM((width, part), BF16),
-            dma((14 + link_count,)),
+            dma((11 + link_count,)),
             dma((3,)),
             dma((3,)),
             dma((lists,)),
             dma((lists,)),
             dma((pieces,)),
             dma((pieces,)),
+            dma((n_head - 1,)),
+            dma((n_head,)),
             dma((n_head - 1,)),
             dma((n_head,)),
         ],

time: 28.1 us -> 28 us (level)
  the two profiles are of different devices: /device:TPU:1 before, /device:TPU:121 now
where the time goes in v3:
time: 28 us; the launch traced here: 27.9 us
  Pallas kernels  26.2 us (94%)
  local copies, waits for them, and re-layouts  1.67 us (6%)
    pallas_call x1, Pallas kernels, per_device(): pl.pallas_call(functools.partial(layer_kernel, n_dom, n_head), name='laye...  26.2 us
    unnamed x1, local copies, waits for them, and re-layouts  1.67 us

profile of v3, /device:TPU:121, one launch (start us, length us, event | category | flops | bytes accessed | tf_op | source)
XLA Modules:
  0.0 27.9 jit_solution(4378854402384047493)
XLA Ops:
  0.0 26.2 %layer.1 = bf16[1024,128]{1,0:T(8,128)(2,1)} custom-call(bf16[4096,128]{1,0:T(8,128)(2,1)} %feats_in.1, bf16[96,128]{1,0:T(8,128)(2,1)} %bitcast.7, bf16[128,128]{1,0:T(8,128)(2,1)} %wo_in.1, bf16[64,128]{1,0:T(8,128)(2,1)} %bitcast.8, bf16[64,128]{1,0:T(8,128)(2,1)} %w2_in.1, f32[2,128]{1,0:T(2,128)} %gains_in.1, bf16[8,128]{1,0:T(8,128)(2,1)} %vtab_in.1, ...), custom_call_target="tpu_custom_call" | custom-call | tf_op jit(solution)/shard_map/layer/pallas_call | solution.py:439
  26.2 1.7 %copy.14 = bf16[1024,128]{1,0:T(8,128)(2,1)} copy(bf16[1024,128]{1,0:T(8,128)(2,1)} %layer.1) | data formatting | bytes 524288

commit v4 on v3

--- a/solution.py
+++ b/solution.py
@@ -88,7 +88,7 @@
     )
 
 
-def near_block(b, mask, vids, q_rows, k_rows, v_t, vk_h, vv_h, near_out, near_top, near_sum):
+def near_block(b, mask, vids, q_rows, k_rows, vk_h, probs, hub_probs, near_top, near_sum):
     width = q_rows.shape[1]
     heads = width // HEAD_DIM
     n_virt = vk_h.shape[0] // heads
@@ -98,14 +98,14 @@
     bias = jnp.where((mask[here, :] > 0) | (row == col), 0.0, NEG).astype(BF16)
     bias_t = dot_nt(eye, bias)
     zero = jnp.zeros((), BF16)
-    keys, queries, values = k_rows[here, :], q_rows[here, :], v_t[:, here]
-    lane_h, sub_h = lax.rem(iota((BLOCK, width), 1), heads), lax.rem(iota((width, BLOCK), 0), heads)
+    keys, queries = k_rows[here, :], q_rows[here, :]
+    lane_h = lax.rem(iota((BLOCK, width), 1), heads)
     scores = dot_nt(
         keys, jnp.concatenate([jnp.where(lane_h == h, queries, zero) for h in range(heads)], axis=0)
     )
     hub = dot_nt(vk_h[...], queries)
     mine = vids[0:1, here] == iota((n_virt, BLOCK), 0)
-    tops, sums, near_p, hub_p = [], [], [], []
+    tops, sums = [], []
     for h in range(heads):
         near = scores[:, h * BLOCK : (h + 1) * BLOCK] + bias_t
         virt = jnp.where(mine, hub[h * n_virt : (h + 1) * n_virt], NEG)
@@ -116,42 +116,57 @@
         virt = jnp.exp(virt - top)
         tops.append(top)
         sums.append(jnp.sum(near, axis=0, keepdims=True) + jnp.sum(virt, axis=0, keepdims=True))
-        near_p.append(near.astype(BF16))
-        hub_p.append(virt)
+        probs[pl.ds((b * heads + h) * BLOCK, BLOCK), :] = near.astype(BF16)
+        hub_probs[pl.ds((b * heads + h) * n_virt, n_virt), :] = virt
     near_top[:, here] = jnp.concatenate(tops, axis=0)
     near_sum[:, here] = jnp.concatenate(sums, axis=0)
+
+
+def near_values(b, probs, hub_probs, v_t, vv_h, near_out):
+    width = v_t.shape[0]
+    heads = width // HEAD_DIM
+    n_virt = vv_h.shape[1] // heads
+    here = pl.ds(b * BLOCK, BLOCK)
+    values = v_t[:, here]
+    sub_h = lax.rem(iota((width, BLOCK), 0), heads)
+    zero = jnp.zeros((), BF16)
     by_head = jnp.concatenate([jnp.where(sub_h == h, values, zero) for h in range(heads)], axis=1)
-    near_out[:, here] = dot_nn(by_head, jnp.concatenate(near_p, axis=0)) + dot_nn(
-        vv_h[...], jnp.concatenate(hub_p, axis=0).astype(BF16)
-    )
-
-
-def far_chunk(c, size, row_refs, wkv_p, q_t, near_out, near_top, near_sum, attended):
+    near = dot_nn(by_head, probs[pl.ds(b * heads * BLOCK, heads * BLOCK), :])
+    hub = dot_nn(vv_h[...], hub_probs[pl.ds(b * heads * n_virt, heads * n_virt), :].astype(BF16))
+    near_out[:, here] = near + hub
+
+
+def far_chunk(c, size, row_refs, wkv_p, q_t, out, top_ref, sum_ref, attended=None):
     width = q_t.shape[0]
     heads = width // HEAD_DIM
-    at = c * size if isinstance(c, int) else pl.multiple_of(c * size, size)
+    at = c * size
     here = pl.ds(at, size)
     split = (HEAD_DIM, heads, size)
     queries = q_t[:, here].reshape(split)
     wkv = wkv_p[...]
     scored, values = [], []
     for ref, first in row_refs:
-        rows = ref[pl.ds(first + at, size), :].astype(BF16)
-        kv = dot_nt(wkv, rows)
+        kv = dot_nt(wkv, ref[pl.ds(first + at, size), :].astype(BF16))
         keys = kv[0:width].astype(BF16).astype(F32).reshape(split)
         scored.append(jnp.sum(keys * queries, axis=0))
         values.append(kv[width:].reshape(split))
-    top = near_top[:, here]
+    before = top_ref[:, here]
+    top = before
     for s in scored:
         top = jnp.maximum(top, s)
-    shrink = jnp.exp(near_top[:, here] - top)
-    total = near_sum[:, here] * shrink
-    mixed = near_out[:, here].reshape(split) * shrink[None]
+    shrink = jnp.exp(before - top)
+    total = sum_ref[:, here] * shrink
+    mixed = out[:, here].reshape(split) * shrink[None]
     for s, v in zip(scored, values):
         weight = jnp.exp(s - top)
         total = total + weight
         mixed = mixed + v * weight[None]
-    attended[:, here] = (mixed * (1.0 / total)[None]).reshape(width, size).astype(BF16)
+    if attended is None:
+        top_ref[:, here] = top
+        sum_ref[:, here] = total
+        out[:, here] = mixed.reshape(width, size)
+    else:
+        attended[:, here] = (mixed * (1.0 / total)[None]).reshape(width, size).astype(BF16)
 
 
 def ffn_chunk(c, size, own, attended, wo_t, w1_t, w2_t, gain_cols, out):
@@ -219,6 +234,8 @@
     near_top,
     near_sum,
     attended,
+    probs,
+    hub_probs,
     local_sems,
     req_send,
     req_recv,
@@ -264,8 +281,16 @@
 
     q_rows_in, f_rows = wqkv_in.shape[0], w1_in.shape[0]
     got_feats = fetch(0, feats_in, feats)
-    share = send_first.shape[0]
-    got_first = fetch(1, send_in.at[0, core, pl.ds(pl.multiple_of(head * share, share), share)], send_first)
+    direct = halo // 2
+    share = (halo - direct) // n_head
+    got_first = [
+        fetch(1, send_in.at[0, core, pl.ds(0, direct)], send_first.at[pl.ds(0, direct)]),
+        fetch(
+            11 + link_count,
+            send_in.at[0, core, pl.ds(pl.multiple_of(direct + head * share, share), share)],
+            send_first.at[pl.ds(direct, share)],
+        ),
+    ]
     got_second = fetch(2, send_in.at[0, 1 - core], send_second)
     got_weights = [
         fetch(3, wqkv_in, weights.at[head, pl.ds(0, q_rows_in)]),
@@ -309,48 +334,45 @@
 
     sent = []
 
-    def send_chunk(index, at, dst, send, recv, device):
-        slot = len(sent)
-        gather_rows(chunk, index, at, table, staged, 0)
-        packed[slot] = staged[...].astype(BF16)
-        copy = remote(packed.at[slot], dst, send, recv, device)
+    used = [0]
+
+    def send_chunk(rows, index, first, dst, send, recv, device):
+        to = packed.at[pl.ds(used[0], rows)]
+        used[0] += rows
+        gather_rows(rows, index, first, table, staged, 0)
+        to[...] = staged[0:rows, :].astype(BF16)
+        copy = remote(to, dst, send, recv, device)
         copy.start()
         sent.append(copy)
+        return copy
 
     def shared(base, h):
-        return lists.at[pl.ds(pl.multiple_of(base * halo + h * share, share), share)]
-
-    got_first.wait()
-    send_chunk(send_first, 0, shared(1 - core, head), list_send.at[0], list_recv.at[0], {"dom": side})
-    got_second.wait()
-    count = halo // chunk
-    for i in range(count):
-        at = pl.multiple_of(core * halo + i * chunk, chunk)
-        send_chunk(
-            send_second,
-            i * chunk,
-            lists.at[pl.ds(at, chunk)],
-            list_send.at[1 + i],
-            list_recv.at[1 + i],
-            {"dom": peer},
+        return lists.at[pl.ds(pl.multiple_of(base * halo + direct + h * share, share), share)]
+
+    for copy in got_first:
+        copy.wait()
+    to_side = {"dom": side}
+    quarter = send_chunk(
+        share, send_first, direct, shared(1 - core, head), list_send.at[0], list_recv.at[0], to_side
+    )
+    list_copies = []
+    for i in range(direct // chunk):
+        at = pl.multiple_of((1 - core) * halo + i * chunk, chunk)
+        dst = lists.at[pl.ds(at, chunk)]
+        s = 1 + i
+        list_copies.append(
+            send_chunk(chunk, send_first, i * chunk, dst, list_send.at[s], list_recv.at[s], to_side)
         )
-    list_copies = list(sent)
 
     pieces = part // chunk
-    passed = []
-    for m in (1, 2, 0):
-        if m == 0:
-            list_copies[0].wait_recv()
-            for k, dev in enumerate(others):
-                copy = remote(
-                    shared(core, head), shared(core, head), pass_send.at[k], pass_recv.at[head], {"head": dev}
-                )
-                copy.start()
-                passed.append(copy)
+    row_copies = {}
+
+    def serve(m):
         requests[m].wait_recv()
         for i in range(pieces):
             s = m * pieces + i
-            send_chunk(
+            row_copies[m, i] = send_chunk(
+                chunk,
                 wanted,
                 m * part + i * chunk,
                 matched.at[m, pl.ds(i * chunk, chunk)],
@@ -359,6 +381,28 @@
                 {"dom": partners[m]},
             )
 
+    serve(1)
+    quarter.wait_recv()
+    passed = []
+    for k, dev in enumerate(others):
+        copy = remote(
+            shared(core, head), shared(core, head), pass_send.at[k], pass_recv.at[head], {"head": dev}
+        )
+        copy.start()
+        passed.append(copy)
+    serve(2)
+    got_second.wait()
+    for i in range(halo // chunk):
+        at = pl.multiple_of(core * halo + i * chunk, chunk)
+        dst = lists.at[pl.ds(at, chunk)]
+        s = 1 + direct // chunk + i
+        list_copies.append(
+            send_chunk(
+                chunk, send_second, i * chunk, dst, list_send.at[s], list_recv.at[s], {"dom": peer}
+            )
+        )
+    serve(0)
+
     for dev in others:
         remote(weights.at[head], weights.at[dev], w_send.at[0], w_recv.at[dev], {"head": dev}).wait_recv()
     for copy in got_rest:
@@ -368,24 +412,31 @@
         q_rows, k_rows, q_t, v_t, vk_h, vv_h,
     )
     for b in range(part // BLOCK):
-        near_block(b, mask, vids, q_rows, k_rows, v_t, vk_h, vv_h, near_out, near_top, near_sum)
+        near_block(b, mask, vids, q_rows, k_rows, vk_h, probs, hub_probs, near_top, near_sum)
+    for b in range(part // BLOCK):
+        near_values(b, probs, hub_probs, v_t, vv_h, near_out)
 
     for dev in others:
         remote(
             shared(core, head), shared(core, dev), pass_send.at[0], pass_recv.at[dev], {"head": dev}
         ).wait_recv()
-    for copy in list_copies[1:]:
+    for copy in list_copies:
         copy.wait_recv()
     widen(lists, 0, table, 0, 2 * halo)
     for copy in got_links:
         copy.wait()
     gather_rows(link_count * part, links, 0, table, far, 0)
 
-    for copy in sent[len(list_copies) :]:
-        copy.wait_recv()
-    row_refs = [(far, e * part) for e in range(link_count)] + [(matched.at[m], 0) for m in range(3)]
+    for m in (0, 2):
+        for i in range(pieces):
+            row_copies[m, i].wait_recv()
+    row_refs = [(far, e * part) for e in range(link_count)] + [(matched.at[m], 0) for m in (0, 2)]
     for c in range(part // 256):
-        far_chunk(c, 256, row_refs, wkv_p, q_t, near_out, near_top, near_sum, attended)
+        far_chunk(c, 256, row_refs, wkv_p, q_t, near_out, near_top, near_sum)
+    for i in range(pieces):
+        row_copies[1, i].wait_recv()
+    for c in range(part // 256):
+        far_chunk(c, 256, [(matched.at[1], 0)], wkv_p, q_t, near_out, near_top, near_sum, attended)
     own_base = pl.multiple_of(head * part, part)
     ffn_chunk(
         0,
@@ -431,8 +482,9 @@
     link_count = links.shape[0]
     vids = virtual_ids.reshape(1, nodes)
     chunk = CHUNK
-    share = halo // n_head
-    lists = 1 + halo // chunk
+    direct = halo // 2
+    share = (halo - direct) // n_head
+    lists = 1 + direct // chunk + halo // chunk
     pieces = 3 * part // chunk
     i32 = jnp.int32
     dma = pltpu.SemaphoreType.DMA
@@ -446,14 +498,14 @@
             pltpu.VMEM((nodes, width), BF16),
             pltpu.VMEM((nodes, width), F32),
             pltpu.VMEM((chunk, width), F32),
-            pltpu.VMEM((lists + pieces, chunk, width), BF16),
+            pltpu.VMEM((share + direct + halo + 3 * part, width), BF16),
             pltpu.VMEM((n_head, w_rows, width), BF16),
             pltpu.VMEM((width, width), BF16),
             pltpu.VMEM((2, width), F32),
             pltpu.VMEM((n_virt, width), BF16),
             pltpu.VMEM((part, BLOCK), i32),
             pltpu.VMEM((1, part), i32),
-            pltpu.SMEM((share,), i32),
+            pltpu.SMEM((direct + share,), i32),
             pltpu.SMEM((halo,), i32),
             pltpu.SMEM((link_count * part,), i32),
             pltpu.SMEM((3 * part,), i32),
@@ -476,7 +528,9 @@
             pltpu.VMEM((heads, part), F32),
             pltpu.VMEM((heads, part), F32),
             pltpu.VMEM((width, part), BF16),
-            dma((11 + link_count,)),
+            pltpu.VMEM((heads * part, BLOCK), BF16),
+            pltpu.VMEM((heads * n_virt * part // BLOCK, BLOCK), F32),
+            dma((12 + link_count,)),
             dma((3,)),
             dma((3,)),
             dma((lists,)),

time: 28 us -> 25.3 us (0.904)
  the two profiles are of different devices: /device:TPU:121 before, /device:TPU:0 now
where the time goes in v4:
time: 25.3 us; the launch traced here: 25.1 us
  Pallas kernels  23.5 us (93%)
  local copies, waits for them, and re-layouts  1.67 us (7%)
    pallas_call x1, Pallas kernels, per_device(): pl.pallas_call(functools.partial(layer_kernel, n_dom, n_head), name='laye...  23.5 us
    unnamed x1, local copies, waits for them, and re-layouts  1.67 us

profile of v4, /device:TPU:0, one launch (start us, length us, event | category | flops | bytes accessed | tf_op | source)
XLA Modules:
  0.0 25.1 jit_solution(7978482325282754676)
XLA Ops:
  0.0 23.5 %layer.1 = bf16[1024,128]{1,0:T(8,128)(2,1)} custom-call(bf16[4096,128]{1,0:T(8,128)(2,1)} %feats_in.1, bf16[96,128]{1,0:T(8,128)(2,1)} %bitcast.7, bf16[128,128]{1,0:T(8,128)(2,1)} %wo_in.1, bf16[64,128]{1,0:T(8,128)(2,1)} %bitcast.8, bf16[64,128]{1,0:T(8,128)(2,1)} %w2_in.1, f32[2,128]{1,0:T(2,128)} %gains_in.1, bf16[8,128]{1,0:T(8,128)(2,1)} %vtab_in.1, ...), custom_call_target="tpu_custom_call" | custom-call | tf_op jit(solution)/shard_map/layer/pallas_call | solution.py:491
  23.5 1.7 %copy.14 = bf16[1024,128]{1,0:T(8,128)(2,1)} copy(bf16[1024,128]{1,0:T(8,128)(2,1)} %layer.1) | data formatting | bytes 524288

commit v5 on v4

--- a/solution.py
+++ b/solution.py
@@ -10,6 +10,7 @@
 HEAD_DIM = 16
 BLOCK = 128
 CHUNK = 512
+PIECE = 512
 MESH = pl.DeviceIdType.MESH
 F32 = jnp.float32
 BF16 = jnp.bfloat16
@@ -50,7 +51,7 @@
     return shifted * lax.rsqrt(second + 1e-05) * gain
 
 
-def prepare(weights, wo, gains, vtab, own, wq_p, wkv_p, w1_t, w2_t, wo_t, gain_cols, q_rows, k_rows, q_t, v_t, vk_h, vv_h):
+def prepare(weights, wo, gains, vtab, own, wq_p, wkv_p, w1_t, w2_t, wo_t, gain_cols, q_rows, k_rows, q_t, own_t, v_t, vk_h, vv_h):
     n_head, _, width = weights.shape
     local = width // n_head
     heads = width // HEAD_DIM
@@ -76,6 +77,7 @@
     q_rows[...] = dot_nt(own, wq).astype(BF16)
     k_rows[...] = dot_nt(own, wk).astype(BF16)
     q_t[...] = dot_nt(wq, own).astype(BF16).astype(F32)
+    own_t[...] = dot_nt(eye, own)
     v_t[...] = dot_nt(wv, own).astype(BF16)
     vk = dot_nt(vtab, wk).astype(BF16)
     vv = dot_nt(wv, vtab).astype(BF16)
@@ -169,13 +171,12 @@
         attended[:, here] = (mixed * (1.0 / total)[None]).reshape(width, size).astype(BF16)
 
 
-def ffn_chunk(c, size, own, attended, wo_t, w1_t, w2_t, gain_cols, out):
+def ffn_chunk(c, size, own_t, attended, wo_t, w1_t, w2_t, gain_cols, out):
     width = attended.shape[0]
     at = c * size if isinstance(c, int) else pl.multiple_of(c * size, size)
     here = pl.ds(at, size)
-    eye = (iota((width, width), 0) == iota((width, width), 1)).astype(BF16)
     gain = [jnp.concatenate([gain_cols[g]] * (size // width), axis=1) for g in (0, 1)]
-    residual = dot_nt(eye, own(here)) + dot_nn(wo_t[...], attended[:, here])
+    residual = own_t[:, here] + dot_nn(wo_t[...], attended[:, here])
     hidden = layer_norm_cols(residual, gain[0]).astype(BF16)
     inner = jax.nn.gelu(dot_nn(w1_t[...], hidden), approximate=True).astype(BF16)
     summed = layer_norm_cols(hidden.astype(F32) + dot_nn(w2_t[...], inner), gain[1])
@@ -227,6 +228,7 @@
     q_rows,
     k_rows,
     q_t,
+    own_t,
     v_t,
     vk_h,
     vv_h,
@@ -281,13 +283,13 @@
 
     q_rows_in, f_rows = wqkv_in.shape[0], w1_in.shape[0]
     got_feats = fetch(0, feats_in, feats)
-    direct = halo // 2
+    direct = halo // 4
     share = (halo - direct) // n_head
     got_first = [
         fetch(1, send_in.at[0, core, pl.ds(0, direct)], send_first.at[pl.ds(0, direct)]),
         fetch(
             11 + link_count,
-            send_in.at[0, core, pl.ds(pl.multiple_of(direct + head * share, share), share)],
+            send_in.at[0, core, pl.ds(pl.multiple_of(direct + head * share, 128), share)],
             send_first.at[pl.ds(direct, share)],
         ),
     ]
@@ -347,7 +349,7 @@
         return copy
 
     def shared(base, h):
-        return lists.at[pl.ds(pl.multiple_of(base * halo + direct + h * share, share), share)]
+        return lists.at[pl.ds(pl.multiple_of(base * halo + direct + h * share, 128), share)]
 
     for copy in got_first:
         copy.wait()
@@ -364,33 +366,23 @@
             send_chunk(chunk, send_first, i * chunk, dst, list_send.at[s], list_recv.at[s], to_side)
         )
 
-    pieces = part // chunk
+    pieces = part // PIECE
     row_copies = {}
 
-    def serve(m):
-        requests[m].wait_recv()
-        for i in range(pieces):
-            s = m * pieces + i
-            row_copies[m, i] = send_chunk(
-                chunk,
-                wanted,
-                m * part + i * chunk,
-                matched.at[m, pl.ds(i * chunk, chunk)],
-                rows_send.at[s],
-                rows_recv.at[s],
-                {"dom": partners[m]},
-            )
-
-    serve(1)
-    quarter.wait_recv()
-    passed = []
-    for k, dev in enumerate(others):
-        copy = remote(
-            shared(core, head), shared(core, head), pass_send.at[k], pass_recv.at[head], {"head": dev}
-        )
-        copy.start()
-        passed.append(copy)
-    serve(2)
+    def serve(m, i):
+        if i == 0:
+            requests[m].wait_recv()
+        s = m * pieces + i
+        row_copies[m, i] = send_chunk(
+            PIECE,
+            wanted,
+            m * part + i * PIECE,
+            matched.at[m, pl.ds(i * PIECE, PIECE)],
+            rows_send.at[s],
+            rows_recv.at[s],
+            {"dom": partners[m]},
+        )
+
     got_second.wait()
     for i in range(halo // chunk):
         at = pl.multiple_of(core * halo + i * chunk, chunk)
@@ -401,7 +393,22 @@
                 chunk, send_second, i * chunk, dst, list_send.at[s], list_recv.at[s], {"dom": peer}
             )
         )
-    serve(0)
+
+    serve(1, 0)
+    serve(2, 0)
+    quarter.wait_recv()
+    passed = []
+    for k, dev in enumerate(others):
+        copy = remote(
+            shared(core, head), shared(core, head), pass_send.at[k], pass_recv.at[head], {"head": dev}
+        )
+        copy.start()
+        passed.append(copy)
+    for i in range(1, pieces):
+        serve(1, i)
+        serve(2, i)
+    for i in range(pieces):
+        serve(0, i)
 
     for dev in others:
         remote(weights.at[head], weights.at[dev], w_send.at[0], w_recv.at[dev], {"head": dev}).wait_recv()
@@ -409,39 +416,44 @@
         copy.wait()
     prepare(
         weights, wo, gains, vtab[...], feats[mine, :], wq_p, wkv_p, w1_t, w2_t, wo_t, gain_cols,
-        q_rows, k_rows, q_t, v_t, vk_h, vv_h,
+        q_rows, k_rows, q_t, own_t, v_t, vk_h, vv_h,
     )
     for b in range(part // BLOCK):
         near_block(b, mask, vids, q_rows, k_rows, vk_h, probs, hub_probs, near_top, near_sum)
     for b in range(part // BLOCK):
         near_values(b, probs, hub_probs, v_t, vv_h, near_out)
 
+    for copy in list_copies:
+        copy.wait_recv()
+    from_peer = pl.multiple_of((1 - core) * halo, halo)
+    from_side = pl.multiple_of(core * halo, halo)
+    widen(lists, from_peer, table, from_peer, halo)
+    widen(lists, from_side, table, from_side, direct)
     for dev in others:
         remote(
             shared(core, head), shared(core, dev), pass_send.at[0], pass_recv.at[dev], {"head": dev}
         ).wait_recv()
-    for copy in list_copies:
-        copy.wait_recv()
-    widen(lists, 0, table, 0, 2 * halo)
+    passed_on = pl.multiple_of(core * halo + direct, chunk)
+    widen(lists, passed_on, table, passed_on, halo - direct)
     for copy in got_links:
         copy.wait()
     gather_rows(link_count * part, links, 0, table, far, 0)
 
-    for m in (0, 2):
+    for i in range(pieces):
+        row_copies[0, i].wait_recv()
+    row_refs = [(far, e * part) for e in range(link_count)] + [(matched.at[0], 0)]
+    for c in range(part // 256):
+        far_chunk(c, 256, row_refs, wkv_p, q_t, near_out, near_top, near_sum)
+    for m in (2, 1):
         for i in range(pieces):
             row_copies[m, i].wait_recv()
-    row_refs = [(far, e * part) for e in range(link_count)] + [(matched.at[m], 0) for m in (0, 2)]
+    row_refs = [(matched.at[m], 0) for m in (1, 2)]
     for c in range(part // 256):
-        far_chunk(c, 256, row_refs, wkv_p, q_t, near_out, near_top, near_sum)
-    for i in range(pieces):
-        row_copies[1, i].wait_recv()
-    for c in range(part // 256):
-        far_chunk(c, 256, [(matched.at[1], 0)], wkv_p, q_t, near_out, near_top, near_sum, attended)
-    own_base = pl.multiple_of(head * part, part)
+        far_chunk(c, 256, row_refs, wkv_p, q_t, near_out, near_top, near_sum, attended)
     ffn_chunk(
         0,
         part,
-        lambda here: feats[pl.ds(own_base + here.start, here.size), :],
+        own_t,
         attended,
         wo_t,
         w1_t,
@@ -482,10 +494,10 @@
     link_count = links.shape[0]
     vids = virtual_ids.reshape(1, nodes)
     chunk = CHUNK
-    direct = halo // 2
+    direct = halo // 4
     share = (halo - direct) // n_head
     lists = 1 + direct // chunk + halo // chunk
-    pieces = 3 * part // chunk
+    pieces = 3 * part // PIECE
     i32 = jnp.int32
     dma = pltpu.SemaphoreType.DMA
     return pl.pallas_call(
@@ -520,6 +532,7 @@
             pltpu.VMEM((2, width, width), F32),
             pltpu.VMEM((part, width), BF16),
             pltpu.VMEM((part, width), BF16),
+            pltpu.VMEM((width, part), F32),
             pltpu.VMEM((width, part), F32),
             pltpu.VMEM((width, part), BF16),
             pltpu.VMEM((heads * n_virt, width), BF16),

time: 25.3 us -> 24.4 us (0.964)
  Pallas kernels: 23.5 us -> 22.6 us
    pallas_call x1, Pallas kernels: 23.5 us -> 22.6 us  [per_device(): pl.pallas_call(functools.partial(layer_kernel, n_dom, n_head), name='laye...]
where the time goes in v5:
time: 24.4 us; the launch traced here: 24.3 us
  Pallas kernels  22.6 us (93%)
  local copies, waits for them, and re-layouts  1.67 us (7%)
    pallas_call x1, Pallas kernels, per_device(): pl.pallas_call(functools.partial(layer_kernel, n_dom, n_head), name='laye...  22.6 us
    unnamed x1, local copies, waits for them, and re-layouts  1.67 us

profile of v5, /device:TPU:0, one launch (start us, length us, event | category | flops | bytes accessed | tf_op | source)
XLA Modules:
  0.0 24.3 jit_solution(15099609757265568736)
XLA Ops:
  0.0 22.6 %layer.1 = bf16[1024,128]{1,0:T(8,128)(2,1)} custom-call(bf16[4096,128]{1,0:T(8,128)(2,1)} %feats_in.1, bf16[96,128]{1,0:T(8,128)(2,1)} %bitcast.7, bf16[128,128]{1,0:T(8,128)(2,1)} %wo_in.1, bf16[64,128]{1,0:T(8,128)(2,1)} %bitcast.8, bf16[64,128]{1,0:T(8,128)(2,1)} %w2_in.1, f32[2,128]{1,0:T(2,128)} %gains_in.1, bf16[8,128]{1,0:T(8,128)(2,1)} %vtab_in.1, ...), custom_call_target="tpu_custom_call" | custom-call | tf_op jit(solution)/shard_map/layer/pallas_call | solution.py:503
  22.6 1.7 %copy.14 = bf16[1024,128]{1,0:T(8,128)(2,1)} copy(bf16[1024,128]{1,0:T(8,128)(2,1)} %layer.1) | data formatting | bytes 524288

commit v6 on v5

--- a/solution.py
+++ b/solution.py
@@ -299,6 +299,27 @@
         fetch(4, w1_in, weights.at[head, pl.ds(q_rows_in, f_rows)]),
         fetch(5, w2_in, weights.at[head, pl.ds(q_rows_in + f_rows, f_rows)]),
     ]
+    def remote(src, dst, send, recv, device):
+        return pltpu.make_async_remote_copy(
+            src_ref=src, dst_ref=dst, send_sem=send, recv_sem=recv, device_id=device, device_id_type=MESH
+        )
+
+    pl.semaphore_wait(barrier, 4 + len(others))
+    requests = {}
+    for m in (1, 2, 0):
+        copy = remote(
+            perm_in.at[m, 0, mine], wanted.at[pl.ds(m * part, part)], req_send.at[m], req_recv.at[m], {"dom": partners[m]}
+        )
+        copy.start()
+        requests[m] = copy
+    for copy in got_weights:
+        copy.wait()
+    w_copies = []
+    for k, dev in enumerate(others):
+        copy = remote(weights.at[head], weights.at[head], w_send.at[k], w_recv.at[head], {"head": dev})
+        copy.start()
+        w_copies.append(copy)
+
     got_rest = [
         fetch(6, wo_in, wo),
         fetch(7, gains_in, gains),
@@ -309,27 +330,6 @@
     got_links = [
         fetch(11 + e, links_in.at[e, mine], links.at[pl.ds(e * part, part)]) for e in range(link_count)
     ]
-
-    def remote(src, dst, send, recv, device):
-        return pltpu.make_async_remote_copy(
-            src_ref=src, dst_ref=dst, send_sem=send, recv_sem=recv, device_id=device, device_id_type=MESH
-        )
-
-    pl.semaphore_wait(barrier, 4 + len(others))
-    requests = []
-    for m in range(3):
-        copy = remote(
-            perm_in.at[m, 0, mine], wanted.at[pl.ds(m * part, part)], req_send.at[m], req_recv.at[m], {"dom": partners[m]}
-        )
-        copy.start()
-        requests.append(copy)
-    for copy in got_weights:
-        copy.wait()
-    w_copies = []
-    for k, dev in enumerate(others):
-        copy = remote(weights.at[head], weights.at[head], w_send.at[k], w_recv.at[head], {"head": dev})
-        copy.start()
-        w_copies.append(copy)
 
     got_feats.wait()
     widen(feats, 0, table, 0, nodes)
@@ -394,8 +394,6 @@
             )
         )
 
-    serve(1, 0)
-    serve(2, 0)
     quarter.wait_recv()
     passed = []
     for k, dev in enumerate(others):
@@ -404,7 +402,7 @@
         )
         copy.start()
         passed.append(copy)
-    for i in range(1, pieces):
+    for i in range(pieces):
         serve(1, i)
         serve(2, i)
     for i in range(pieces):
@@ -461,7 +459,7 @@
         gain_cols,
         out,
     )
-    for copy in requests + w_copies + sent + passed:
+    for copy in list(requests.values()) + w_copies + sent + passed:
         copy.wait_send()
 
 

time: 24.4 us -> 24.4 us (level)
  no operation moved by 1% of the time
where the time goes in v6:
time: 24.4 us; the launch traced here: 24.3 us
  Pallas kernels  22.6 us (93%)
  local copies, waits for them, and re-layouts  1.67 us (7%)
    pallas_call x1, Pallas kernels, per_device(): pl.pallas_call(functools.partial(layer_kernel, n_dom, n_head), name='laye...  22.6 us
    unnamed x1, local copies, waits for them, and re-layouts  1.67 us

profile of v6, /device:TPU:0, one launch (start us, length us, event | category | flops | bytes accessed | tf_op | source)
XLA Modules:
  0.0 24.3 jit_solution(8916289694619870241)
XLA Ops:
  0.0 22.6 %layer.1 = bf16[1024,128]{1,0:T(8,128)(2,1)} custom-call(bf16[4096,128]{1,0:T(8,128)(2,1)} %feats_in.1, bf16[96,128]{1,0:T(8,128)(2,1)} %bitcast.7, bf16[128,128]{1,0:T(8,128)(2,1)} %wo_in.1, bf16[64,128]{1,0:T(8,128)(2,1)} %bitcast.8, bf16[64,128]{1,0:T(8,128)(2,1)} %w2_in.1, f32[2,128]{1,0:T(2,128)} %gains_in.1, bf16[8,128]{1,0:T(8,128)(2,1)} %vtab_in.1, ...), custom_call_target="tpu_custom_call" | custom-call | tf_op jit(solution)/shard_map/layer/pallas_call | solution.py:501
  22.6 1.7 %copy.14 = bf16[1024,128]{1,0:T(8,128)(2,1)} copy(bf16[1024,128]{1,0:T(8,128)(2,1)} %layer.1) | data formatting | bytes 524288

commit v7 on v6

--- a/solution.py
+++ b/solution.py
@@ -435,12 +435,12 @@
     widen(lists, passed_on, table, passed_on, halo - direct)
     for copy in got_links:
         copy.wait()
-    gather_rows(link_count * part, links, 0, table, far, 0)
-
     for i in range(pieces):
         row_copies[0, i].wait_recv()
     row_refs = [(far, e * part) for e in range(link_count)] + [(matched.at[0], 0)]
     for c in range(part // 256):
+        for e in range(link_count):
+            gather_rows(256, links, e * part + c * 256, table, far, e * part + c * 256)
         far_chunk(c, 256, row_refs, wkv_p, q_t, near_out, near_top, near_sum)
     for m in (2, 1):
         for i in range(pieces):

time: 24.4 us -> 24.7 us (1.012)
  Pallas kernels: 22.6 us -> 22.9 us
    pallas_call x1, Pallas kernels: 22.6 us -> 22.9 us  [per_device(): pl.pallas_call(functools.partial(layer_kernel, n_dom, n_head), name='laye...]
where the time goes in v7:
time: 24.7 us; the launch traced here: 24.6 us
  Pallas kernels  22.9 us (93%)
  local copies, waits for them, and re-layouts  1.67 us (7%)
    pallas_call x1, Pallas kernels, per_device(): pl.pallas_call(functools.partial(layer_kernel, n_dom, n_head), name='laye...  22.9 us
    unnamed x1, local copies, waits for them, and re-layouts  1.67 us

profile of v7, /device:TPU:0, one launch (start us, length us, event | category | flops | bytes accessed | tf_op | source)
XLA Modules:
  0.0 24.6 jit_solution(8113269338862466322)
XLA Ops:
  0.0 22.9 %layer.1 = bf16[1024,128]{1,0:T(8,128)(2,1)} custom-call(bf16[4096,128]{1,0:T(8,128)(2,1)} %feats_in.1, bf16[96,128]{1,0:T(8,128)(2,1)} %bitcast.7, bf16[128,128]{1,0:T(8,128)(2,1)} %wo_in.1, bf16[64,128]{1,0:T(8,128)(2,1)} %bitcast.8, bf16[64,128]{1,0:T(8,128)(2,1)} %w2_in.1, f32[2,128]{1,0:T(2,128)} %gains_in.1, bf16[8,128]{1,0:T(8,128)(2,1)} %vtab_in.1, ...), custom_call_target="tpu_custom_call" | custom-call | tf_op jit(solution)/shard_map/layer/pallas_call | solution.py:501
  22.9 1.7 %copy.14 = bf16[1024,128]{1,0:T(8,128)(2,1)} copy(bf16[1024,128]{1,0:T(8,128)(2,1)} %layer.1) | data formatting | bytes 524288
